TPU v7x, 32 devices: a whole 2x2x4 slice. The times are simulated.
32 devices in a mesh: lon: 8 (over z, core), lat: 4 (over y, x).
Axes of the slice: x: 2, y: 2, z: 4, core: 2. Of those that a mesh axis runs over, the one named last changes fastest.
Arguments:
- tracers: float32 [2, 10, 256, 1024], P(None, None, 'lat', 'lon'), may hold values from -6 to 6
- velocity: float32 [2, 10, 256, 1024], P(None, None, 'lat', 'lon'), may hold values from -6 to 6
- active_levels: int32 [256, 1024], P('lat', 'lon'), may hold values from 0 to 10, as said below
- diffusivity: float32 [256, 1024], P('lat', 'lon'), may hold values from 0.02 to 0.2
- viscosity: float32 [256, 1024], P('lat', 'lon'), may hold values from 0.002 to 0.012
- ocean_depth: float32 [256, 1024], P('lat', 'lon'), may hold values from 0.5 to 1.5
- wind_forcing: float32 [2, 256, 1024], P(None, 'lat', 'lon'), may hold values from -5 to 5
Outputs:
- tracers_out: float32 [2, 10, 256, 1024], P(None, None, 'lat', 'lon')
- velocity_out: float32 [2, 10, 256, 1024], P(None, None, 'lat', 'lon')
- surface: float32 [256, 1024], P('lat', 'lon')
Inputs may be any that keep to these rules, and one draw needn't show every extreme that they name: `active_levels`: 0 marks land, which covers whole aligned blocks of 8 x 8 cells; every other cell has 1 to 10 wet levels.
All inputs are finite; a program needn't handle non-finite values.
Results may differ from a plain program's by a relative error of at most 0.0003.
Values sent between devices are 32-bit elements; how exact they have to be, the bound alone decides.
A program may use at most 128 MiB of HBM per device.

v0:
```python
import math

import jax
import jax.numpy as jnp
from jax import lax
from jax.sharding import PartitionSpec as P

SUBCYCLES = 8
SOLVE_ITERS = 4


edge_offsets = ((0, 1), (0, -1), (1, 0), (-1, 0))
corner_offsets = ((1, 1), (1, -1), (-1, 1), (-1, -1))
flow_step = 0.3
slope_step = 0.3
floor_diag = 0.05


def extended(block, sides, width):
    for axis, dim in sides:
        count = lax.axis_size(axis)
        forward = [(i, i + 1) for i in range(count - 1)]
        forward.append((count - 1, 0))
        backward = [(target, source) for source, target in forward]
        low = lax.ppermute(
            lax.slice_in_dim(block, block.shape[dim] - width, None, axis=dim), axis, forward
        )
        high = lax.ppermute(lax.slice_in_dim(block, 0, width, axis=dim), axis, backward)
        block = jnp.concatenate([low, block, high], axis=dim)
    return block


def from_partner(array, axis, apart):
    return lax.ppermute(array, axis, [(i, i ^ 1 << apart) for i in range(lax.axis_size(axis))])


def parity_of(values):
    return jnp.array(values, jnp.float32).reshape(-1, 1, 1)


def window(field, row_off, col_off):
    row_count = field.shape[-2] - 2
    col_count = field.shape[-1] - 2
    inner = lax.slice_in_dim(field, 1 + row_off, 1 + row_off + row_count, axis=field.ndim - 2)
    return lax.slice_in_dim(inner, 1 + col_off, 1 + col_off + col_count, axis=field.ndim - 1)


def masked_laplacian(field, coefficient, wet_mask):
    centre = window(field, 0, 0)
    mask_centre = window(wet_mask, 0, 0)
    summed = None
    for row_off, col_off in edge_offsets:
        face_weight = mask_centre * window(wet_mask, row_off, col_off)
        if coefficient is not None:
            face_weight = (
                0.5
                * (window(coefficient, 0, 0) + window(coefficient, row_off, col_off))
                * face_weight
            )
        flux_term = face_weight * (window(field, row_off, col_off) - centre)
        summed = flux_term if summed is None else summed + flux_term
    return summed


def clinic_extend(stacked, margin, parity):
    padded = extended(stacked, (("lon", 2), ("lat", 1)), margin)
    rim_rows = padded[:, -2 * margin : -margin, :]
    partner = rim_rows
    for bit_index in range(lax.axis_size("lon").bit_length() - 1):
        partner = from_partner(partner, "lon", bit_index)
    folded = jnp.flip(partner, (1, 2)) * parity
    lat_index = lax.axis_index("lat")
    south_rows = jnp.where(lat_index == 0, jnp.zeros_like(padded[:, :margin]), padded[:, :margin])
    north_rows = jnp.where(lat_index == lax.axis_size("lat") - 1, folded, padded[:, -margin:])
    return jnp.concatenate([south_rows, padded[:, margin:-margin], north_rows], axis=1)


def extend(stacked, margin, parity):
    return clinic_extend(stacked, margin, parity)


def squares(residual):
    return lax.psum(jnp.sum(residual * residual), ("lon", "lat"))


def nine_weights(statics):
    depth_pad = statics[0]
    ocean_pad = statics[1]
    depth_centre = window(depth_pad, 0, 0)
    ocean_centre = window(ocean_pad, 0, 0)
    weights = []
    for offsets, scale in ((edge_offsets, 1.0), (corner_offsets, 0.5)):
        for row_off, col_off in offsets:
            weights.append(
                scale
                * 0.5
                * (depth_centre + window(depth_pad, row_off, col_off))
                * ocean_centre
                * window(ocean_pad, row_off, col_off)
            )
    diagonal = floor_diag * ocean_centre + (1.0 - ocean_centre)
    return (weights, diagonal)


def operate_nine(direction_pad, weights, diagonal):
    centre = window(direction_pad, 0, 0)
    summed = diagonal * centre
    for offset, weight in zip(edge_offsets + corner_offsets, weights):
        summed = summed + weight * (centre - window(direction_pad, offset[0], offset[1]))
    return summed


def barotropic(fields):
    start_east, start_north, ocean_depth, ocean_mask = (fields[0], fields[1], fields[2], fields[3])
    height = jnp.zeros_like(start_east)
    east_flow, north_flow = (start_east, start_north)
    statics = extend(jnp.stack([ocean_depth, ocean_mask]), 1, parity_of([1.0, 1.0]))
    depth_pad = statics[0]
    for cycle_index in range(SUBCYCLES):
        moved = extend(jnp.stack([east_flow, north_flow]), 1, parity_of([-1.0, -1.0]))
        flux_east = depth_pad * moved[0]
        flux_north = depth_pad * moved[1]
        divergence = 0.5 * (
            window(flux_east, 0, 1)
            - window(flux_east, 0, -1)
            + (window(flux_north, 1, 0) - window(flux_north, -1, 0))
        )
        height = height - flow_step * ocean_mask * divergence
        height_pad = extend(height[None], 1, parity_of([1.0]))[0]
        east_flow = east_flow - slope_step * ocean_mask * (
            0.5 * (window(height_pad, 0, 1) - window(height_pad, 0, -1))
        )
        north_flow = north_flow - slope_step * ocean_mask * (
            0.5 * (window(height_pad, 1, 0) - window(height_pad, -1, 0))
        )
    weights, diagonal = nine_weights(statics)
    surface = jnp.zeros_like(height)
    residual = height
    direction = height
    old_norm = squares(residual)
    for iteration in range(SOLVE_ITERS):
        direction_pad = extend(direction[None], 1, parity_of([1.0]))[0]
        image = operate_nine(direction_pad, weights, diagonal)
        step_size = old_norm / lax.psum(jnp.sum(direction * image), ("lon", "lat"))
        surface = surface + step_size * direction
        residual = residual - step_size * image
        new_norm = squares(residual)
        direction = residual + new_norm / old_norm * direction
        old_norm = new_norm
    surface_pad = extend(surface[None], 1, parity_of([1.0]))[0]
    east_final = east_flow - slope_step * ocean_mask * (
        0.5 * (window(surface_pad, 0, 1) - window(surface_pad, 0, -1))
    )
    north_final = north_flow - slope_step * ocean_mask * (
        0.5 * (window(surface_pad, 1, 0) - window(surface_pad, -1, 0))
    )
    return jnp.stack([east_final, north_final, surface])


def per_device(tracers, velocity, active_levels, diffusivity, viscosity, ocean_depth, wind_forcing):
    level_total = tracers.shape[1]
    row_count = tracers.shape[2]
    col_count = tracers.shape[3]
    levels_float = active_levels.astype(jnp.float32)
    stacked = jnp.concatenate(
        [
            tracers.reshape(2 * level_total, row_count, col_count),
            velocity.reshape(2 * level_total, row_count, col_count),
            jnp.stack([diffusivity, viscosity, levels_float]),
        ],
        axis=0,
    )
    parity = jnp.concatenate(
        [
            jnp.ones((2 * level_total,), jnp.float32),
            -jnp.ones((2 * level_total,), jnp.float32),
            jnp.ones((3,), jnp.float32),
        ]
    ).reshape(-1, 1, 1)
    padded = clinic_extend(stacked, 2, parity)
    pad_rows = row_count + 4
    pad_cols = col_count + 4
    tracer_pad = padded[: 2 * level_total].reshape(2, level_total, pad_rows, pad_cols)
    velocity_pad = padded[2 * level_total : 4 * level_total].reshape(
        2, level_total, pad_rows, pad_cols
    )
    diffusion_pad = padded[4 * level_total]
    viscous_pad = padded[4 * level_total + 1]
    levels_pad = padded[4 * level_total + 2]
    level_ids = jnp.arange(level_total, dtype=jnp.float32)[:, None, None]
    wet_pad = (level_ids < levels_pad).astype(jnp.float32)
    tracer_lap = window(masked_laplacian(tracer_pad, diffusion_pad, wet_pad), 0, 0)
    tracers_out = tracers + tracer_lap
    first_pass = masked_laplacian(velocity_pad, None, wet_pad)
    second_pass = masked_laplacian(first_pass, window(viscous_pad, 0, 0), window(wet_pad, 0, 0))
    wet = wet_pad[:, 2:-2, 2:-2]
    row_ids = (lax.axis_index("lat") * row_count + jnp.arange(row_count, dtype=jnp.int32)).astype(
        jnp.float32
    )[:, None]
    coriolis = 0.25 * jnp.sin(
        math.pi * ((row_ids + 0.5) / (row_count * lax.axis_size("lat")) - 0.5)
    )
    rotated = jnp.stack([velocity[1], -velocity[0]])
    star = wet * (velocity - second_pass + coriolis * rotated)
    column_mean = jnp.sum(star, axis=1) / jnp.maximum(levels_float, 1.0)
    ocean_mask = (active_levels > 0).astype(jnp.float32)
    start = column_mean + wind_forcing * ocean_mask
    fields = jnp.stack([start[0], start[1], ocean_depth, ocean_mask])
    result = barotropic(fields)
    velocity_out = star + wet * (result[:2] - column_mean)[:, None]
    return (tracers_out, velocity_out, result[2])


def solution(mesh):
    placed = (
        P(None, None, "lat", "lon"),
        P(None, None, "lat", "lon"),
        P("lat", "lon"),
        P("lat", "lon"),
        P("lat", "lon"),
        P("lat", "lon"),
        P(None, "lat", "lon"),
    )
    return jax.shard_map(
        per_device,
        mesh=mesh,
        in_specs=placed,
        out_specs=(P(None, None, "lat", "lon"), P(None, None, "lat", "lon"), P("lat", "lon")),
        check_vma=False,
    )
```

profile of v0, /device:TPU:0, one launch (start us, length us, event | category | flops | bytes accessed | tf_op | source)
XLA Modules:
  0.0 719.7 jit_solution(5913157737257406666)
XLA Ops:
  4.1 4.0 collective-permute-start.8
  35.5 5.4 collective-permute-done.5
  53.0 3.5 collective-permute-start.15
  68.8 4.2 collective-permute-done.19
  74.5 3.5 collective-permute-start.22
  91.5 3.5 collective-permute-start.29
  107.7 3.5 collective-permute-start.36
  124.6 3.5 collective-permute-start.43
  140.7 3.5 collective-permute-start.50
  157.7 3.5 collective-permute-start.57
  173.7 3.5 collective-permute-start.64
  190.7 3.5 collective-permute-start.71
  206.8 3.5 collective-permute-start.78
  223.7 3.5 collective-permute-start.85
  239.8 3.5 collective-permute-start.92
  256.8 3.5 collective-permute-start.99
  272.8 3.5 collective-permute-start.106
  289.8 3.5 collective-permute-start.113
  306.7 3.7 collective-permute-start.120
  327.8 39.7 %all-reduce = (f32[]{:T(128)}, f32[]{:T(128)}) all-reduce(f32[]{:T(128)} %get-tuple-element.7, f32[]{:T(128)} %get-tuple-element.6), channel_id=1, replica_groups=mesh['lon'=8,'lat'=4] {'lon','lat'}, use_global_device_ids=true, to_apply=%region_2.3 | all-reduce | flops 2 | bytes 16 | tf_op jit(solution)/shard_map/psum | solution.py:83
  369.4 41.4 %psum.58 = f32[]{:T(128)} all-reduce(f32[]{:T(128)} %multiply_reduce_fusion.4), channel_id=1, replica_groups=mesh['lon'=8,'lat'=4] {'lon','lat'}, use_global_device_ids=true, to_apply=%region_6.7 | all-reduce | flops 1 | bytes 8 | tf_op jit(solution)/shard_map/psum | solution.py:83
  412.1 3.5 collective-permute-start.127
  432.1 40.0 %psum.59 = f32[]{:T(128)} all-reduce(f32[]{:T(128)} %get-tuple-element.14), channel_id=1, replica_groups=mesh['lon'=8,'lat'=4] {'lon','lat'}, use_global_device_ids=true, to_apply=%region_8.9 | all-reduce | flops 1 | bytes 8 | tf_op jit(solution)/shard_map/psum | solution.py:144
  475.4 42.3 %psum.60 = f32[]{:T(128)} all-reduce(f32[]{:T(128)} %get-tuple-element.12), channel_id=1, replica_groups=mesh['lon'=8,'lat'=4] {'lon','lat'}, use_global_device_ids=true, to_apply=%region_10.11 | all-reduce | flops 1 | bytes 8 | tf_op jit(solution)/shard_map/psum | solution.py:83
  519.8 3.5 collective-permute-start.134
  539.8 40.0 %psum.61 = f32[]{:T(128)} all-reduce(f32[]{:T(128)} %get-tuple-element.10), channel_id=1, replica_groups=mesh['lon'=8,'lat'=4] {'lon','lat'}, use_global_device_ids=true, to_apply=%region_12.13 | all-reduce | flops 1 | bytes 8 | tf_op jit(solution)/shard_map/psum | solution.py:144
  582.6 42.3 %psum.62 = f32[]{:T(128)} all-reduce(f32[]{:T(128)} %multiply_reduce_fusion), channel_id=1, replica_groups=mesh['lon'=8,'lat'=4] {'lon','lat'}, use_global_device_ids=true, to_apply=%region_14.15 | all-reduce | flops 1 | bytes 8 | tf_op jit(solution)/shard_map/psum | solution.py:83
  627.1 3.5 collective-permute-start.141
  633.7 4.6 fusion.230
  654.2 38.8 %psum.63 = f32[]{:T(128)} all-reduce(f32[]{:T(128)} %fusion.111), channel_id=1, replica_groups=mesh['lon'=8,'lat'=4] {'lon','lat'}, use_global_device_ids=true, to_apply=%region_16.17 | all-reduce | flops 1 | bytes 8 | tf_op jit(solution)/shard_map/psum | solution.py:144
  694.4 3.5 collective-permute-start.148
  700.8 5.1 fusion.20
  (622 shorter events, 328.9 us)
Async XLA Ops:
  3.7 22.9 %collective-permute-start.7 = (f32[2,64,1]{2,1,0:T(8,128)}, f32[2,64,1]{2,1,0:T(8,128)S(1)}, u32[]{:S(2)}, u32[]{:S(2)}) collective-permute-start(f32[2,64,1]{2,1,0:T(8,128)} %get-tuple-element.177), channel_id=1, source_target_pairs={{0,4},{4,8},{8,12},{12,16},{16,20},{20,24},{24,28},{28,0},{1,5},{5... | collective-permute-start | bytes 1544 | tf_op jit(solution)/shard_map/ppermute | solution.py:25
  4.1 22.4 %collective-permute-start.8 = (f32[2,64,1]{2,1,0:T(8,128)}, f32[2,64,1]{2,1,0:T(8,128)}, u32[]{:S(2)}, u32[]{:S(2)}) collective-permute-start(f32[2,64,1]{2,1,0:T(8,128)} %get-tuple-element.178), channel_id=1, source_target_pairs={{4,0},{8,4},{12,8},{16,12},{20,16},{24,20},{28,24},{0,28},{5,1},{9... | collective-permute-start | bytes 1544 | tf_op jit(solution)/shard_map/ppermute | solution.py:28
  13.5 8.6 %collective-permute-start.1 = (f32[43,64,2]{1,2,0:T(2,128)}, f32[43,64,2]{1,2,0:T(2,128)}, u32[]{:S(2)}, u32[]{:S(2)}) collective-permute-start(f32[43,64,2]{1,2,0:T(2,128)} %copy.62), channel_id=1, source_target_pairs={{4,0},{8,4},{12,8},{16,12},{20,16},{24,20},{28,24},{0,28},{5,1},{9... | collective-permute-start | bytes 66056 | tf_op jit(solution)/shard_map/ppermute | solution.py:28
  30.6 28.8 %collective-permute-start.11 = (f32[2,1,130]{2,1,0:T(1,128)}, f32[2,1,130]{2,1,0:T(1,128)}, u32[]{:S(2)}, u32[]{:S(2)}) collective-permute-start(f32[2,1,130]{2,1,0:T(1,128)} %collective-permute-done.10), channel_id=1, source_target_pairs={{0,8},{4,12},{8,0},{12,4},{16,24},{20,28},{24,16},{28,20},{1,9},{5... | collective-permute-start | bytes 3128 | tf_op jit(solution)/shard_map/ppermute | solution.py:34
  32.7 10.1 %collective-permute-start.6 = (f32[43,2,132]{2,1,0:T(2,128)}, f32[43,2,132]{2,1,0:T(2,128)}, u32[]{:S(2)}, u32[]{:S(2)}) collective-permute-start(f32[43,2,132]{2,1,0:T(2,128)} %get-tuple-element.44), channel_id=1, source_target_pairs={{1,0},{2,1},{3,2},{0,3},{5,4},{6,5},{7,6},{4,7},{9,8},{10,9},{11,1... | collective-permute-start | bytes 136232 | tf_op jit(solution)/shard_map/ppermute | solution.py:28
  65.0 8.2 %collective-permute-start.20 = (f32[2,1,130]{2,1,0:T(1,128)S(1)}, f32[2,1,130]{2,1,0:T(1,128)S(1)}, u32[]{:S(2)}, u32[]{:S(2)}) collective-permute-start(f32[2,1,130]{2,1,0:T(1,128)S(1)} %get-tuple-element.100), channel_id=1, source_target_pairs={{1,0},{2,1},{3,2},{0,3},{5,4},{6,5},{7,6},{4,7},{9,8},{10,9},{11,1... | collective-permute-start | bytes 3128 | tf_op jit(solution)/shard_map/ppermute | solution.py:28
  79.8 9.0 %collective-permute-start.27 = (f32[1,1,130]{2,1,0:T(1,128)S(1)}, f32[1,1,130]{2,1,0:T(1,128)S(1)}, u32[]{:S(2)}, u32[]{:S(2)}) collective-permute-start(f32[1,1,130]{2,1,0:T(1,128)S(1)} %get-tuple-element.176), channel_id=1, source_target_pairs={{0,1},{1,2},{2,3},{3,0},{4,5},{5,6},{6,7},{7,4},{8,9},{9,10},{10,1... | collective-permute-start | bytes 1568 | tf_op jit(solution)/shard_map/ppermute | solution.py:25
  82.3 8.8 %collective-permute-start.26 = (f32[1,1,130]{2,1,0:T(1,128)S(1)}, f32[1,1,130]{2,1,0:T(1,128)S(1)}, u32[]{:S(2)}, u32[]{:S(2)}) collective-permute-start(f32[1,1,130]{2,1,0:T(1,128)S(1)} %get-tuple-element.175), channel_id=1, source_target_pairs={{1,0},{2,1},{3,2},{0,3},{5,4},{6,5},{7,6},{4,7},{9,8},{10,9},{11,1... | collective-permute-start | bytes 1568 | tf_op jit(solution)/shard_map/ppermute | solution.py:28
  113.0 9.0 %collective-permute-start.41 = (f32[1,1,130]{2,1,0:T(1,128)S(1)}, f32[1,1,130]{2,1,0:T(1,128)S(1)}, u32[]{:S(2)}, u32[]{:S(2)}) collective-permute-start(f32[1,1,130]{2,1,0:T(1,128)S(1)} %get-tuple-element.172), channel_id=1, source_target_pairs={{0,1},{1,2},{2,3},{3,0},{4,5},{5,6},{6,7},{7,4},{8,9},{9,10},{10,1... | collective-permute-start | bytes 1568 | tf_op jit(solution)/shard_map/ppermute | solution.py:25
  114.0 10.2 %collective-permute-start.40 = (f32[1,1,130]{2,1,0:T(1,128)S(1)}, f32[1,1,130]{2,1,0:T(1,128)S(1)}, u32[]{:S(2)}, u32[]{:S(2)}) collective-permute-start(f32[1,1,130]{2,1,0:T(1,128)S(1)} %get-tuple-element.171), channel_id=1, source_target_pairs={{1,0},{2,1},{3,2},{0,3},{5,4},{6,5},{7,6},{4,7},{9,8},{10,9},{11,1... | collective-permute-start | bytes 1568 | tf_op jit(solution)/shard_map/ppermute | solution.py:28
  146.0 9.0 %collective-permute-start.55 = (f32[1,1,130]{2,1,0:T(1,128)S(1)}, f32[1,1,130]{2,1,0:T(1,128)S(1)}, u32[]{:S(2)}, u32[]{:S(2)}) collective-permute-start(f32[1,1,130]{2,1,0:T(1,128)S(1)} %get-tuple-element.168), channel_id=1, source_target_pairs={{0,1},{1,2},{2,3},{3,0},{4,5},{5,6},{6,7},{7,4},{8,9},{9,10},{10,1... | collective-permute-start | bytes 1568 | tf_op jit(solution)/shard_map/ppermute | solution.py:25
  146.1 11.1 %collective-permute-start.54 = (f32[1,1,130]{2,1,0:T(1,128)S(1)}, f32[1,1,130]{2,1,0:T(1,128)S(1)}, u32[]{:S(2)}, u32[]{:S(2)}) collective-permute-start(f32[1,1,130]{2,1,0:T(1,128)S(1)} %get-tuple-element.167), channel_id=1, source_target_pairs={{1,0},{2,1},{3,2},{0,3},{5,4},{6,5},{7,6},{4,7},{9,8},{10,9},{11,1... | collective-permute-start | bytes 1568 | tf_op jit(solution)/shard_map/ppermute | solution.py:28
  179.0 9.0 %collective-permute-start.69 = (f32[1,1,130]{2,1,0:T(1,128)S(1)}, f32[1,1,130]{2,1,0:T(1,128)S(1)}, u32[]{:S(2)}, u32[]{:S(2)}) collective-permute-start(f32[1,1,130]{2,1,0:T(1,128)S(1)} %get-tuple-element.164), channel_id=1, source_target_pairs={{0,1},{1,2},{2,3},{3,0},{4,5},{5,6},{6,7},{7,4},{8,9},{9,10},{10,1... | collective-permute-start | bytes 1568 | tf_op jit(solution)/shard_map/ppermute | solution.py:25
  179.1 11.1 %collective-permute-start.68 = (f32[1,1,130]{2,1,0:T(1,128)S(1)}, f32[1,1,130]{2,1,0:T(1,128)S(1)}, u32[]{:S(2)}, u32[]{:S(2)}) collective-permute-start(f32[1,1,130]{2,1,0:T(1,128)S(1)} %get-tuple-element.163), channel_id=1, source_target_pairs={{1,0},{2,1},{3,2},{0,3},{5,4},{6,5},{7,6},{4,7},{9,8},{10,9},{11,1... | collective-permute-start | bytes 1568 | tf_op jit(solution)/shard_map/ppermute | solution.py:28
  212.1 9.0 %collective-permute-start.83 = (f32[1,1,130]{2,1,0:T(1,128)S(1)}, f32[1,1,130]{2,1,0:T(1,128)S(1)}, u32[]{:S(2)}, u32[]{:S(2)}) collective-permute-start(f32[1,1,130]{2,1,0:T(1,128)S(1)} %get-tuple-element.160), channel_id=1, source_target_pairs={{0,1},{1,2},{2,3},{3,0},{4,5},{5,6},{6,7},{7,4},{8,9},{9,10},{10,1... | collective-permute-start | bytes 1568 | tf_op jit(solution)/shard_map/ppermute | solution.py:25
  212.1 11.1 %collective-permute-start.82 = (f32[1,1,130]{2,1,0:T(1,128)S(1)}, f32[1,1,130]{2,1,0:T(1,128)S(1)}, u32[]{:S(2)}, u32[]{:S(2)}) collective-permute-start(f32[1,1,130]{2,1,0:T(1,128)S(1)} %get-tuple-element.159), channel_id=1, source_target_pairs={{1,0},{2,1},{3,2},{0,3},{5,4},{6,5},{7,6},{4,7},{9,8},{10,9},{11,1... | collective-permute-start | bytes 1568 | tf_op jit(solution)/shard_map/ppermute | solution.py:28
  245.1 9.0 %collective-permute-start.97 = (f32[1,1,130]{2,1,0:T(1,128)S(1)}, f32[1,1,130]{2,1,0:T(1,128)S(1)}, u32[]{:S(2)}, u32[]{:S(2)}) collective-permute-start(f32[1,1,130]{2,1,0:T(1,128)S(1)} %get-tuple-element.156), channel_id=1, source_target_pairs={{0,1},{1,2},{2,3},{3,0},{4,5},{5,6},{6,7},{7,4},{8,9},{9,10},{10,1... | collective-permute-start | bytes 1568 | tf_op jit(solution)/shard_map/ppermute | solution.py:25
  245.2 11.1 %collective-permute-start.96 = (f32[1,1,130]{2,1,0:T(1,128)S(1)}, f32[1,1,130]{2,1,0:T(1,128)S(1)}, u32[]{:S(2)}, u32[]{:S(2)}) collective-permute-start(f32[1,1,130]{2,1,0:T(1,128)S(1)} %get-tuple-element.155), channel_id=1, source_target_pairs={{1,0},{2,1},{3,2},{0,3},{5,4},{6,5},{7,6},{4,7},{9,8},{10,9},{11,1... | collective-permute-start | bytes 1568 | tf_op jit(solution)/shard_map/ppermute | solution.py:28
  278.2 9.0 %collective-permute-start.111 = (f32[1,1,130]{2,1,0:T(1,128)S(1)}, f32[1,1,130]{2,1,0:T(1,128)S(1)}, u32[]{:S(2)}, u32[]{:S(2)}) collective-permute-start(f32[1,1,130]{2,1,0:T(1,128)S(1)} %get-tuple-element.152), channel_id=1, source_target_pairs={{0,1},{1,2},{2,3},{3,0},{4,5},{5,6},{6,7},{7,4},{8,9},{9,10},{10,1... | collective-permute-start | bytes 1568 | tf_op jit(solution)/shard_map/ppermute | solution.py:25
  278.2 11.1 %collective-permute-start.110 = (f32[1,1,130]{2,1,0:T(1,128)S(1)}, f32[1,1,130]{2,1,0:T(1,128)S(1)}, u32[]{:S(2)}, u32[]{:S(2)}) collective-permute-start(f32[1,1,130]{2,1,0:T(1,128)S(1)} %get-tuple-element.151), channel_id=1, source_target_pairs={{1,0},{2,1},{3,2},{0,3},{5,4},{6,5},{7,6},{4,7},{9,8},{10,9},{11,1... | collective-permute-start | bytes 1568 | tf_op jit(solution)/shard_map/ppermute | solution.py:28
  313.8 9.0 %collective-permute-start.125 = (f32[1,1,130]{2,1,0:T(1,128)S(1)}, f32[1,1,130]{2,1,0:T(1,128)S(1)}, u32[]{:S(2)}, u32[]{:S(2)}) collective-permute-start(f32[1,1,130]{2,1,0:T(1,128)S(1)} %get-tuple-element.148), channel_id=1, source_target_pairs={{0,1},{1,2},{2,3},{3,0},{4,5},{5,6},{6,7},{7,4},{8,9},{9,10},{10,1... | collective-permute-start | bytes 1568 | tf_op jit(solution)/shard_map/ppermute | solution.py:25
  315.3 9.6 %collective-permute-start.124 = (f32[1,1,130]{2,1,0:T(1,128)S(1)}, f32[1,1,130]{2,1,0:T(1,128)S(1)}, u32[]{:S(2)}, u32[]{:S(2)}) collective-permute-start(f32[1,1,130]{2,1,0:T(1,128)S(1)} %get-tuple-element.147), channel_id=1, source_target_pairs={{1,0},{2,1},{3,2},{0,3},{5,4},{6,5},{7,6},{4,7},{9,8},{10,9},{11,1... | collective-permute-start | bytes 1568 | tf_op jit(solution)/shard_map/ppermute | solution.py:28
  417.5 9.0 %collective-permute-start.132 = (f32[1,1,130]{2,1,0:T(1,128)S(1)}, f32[1,1,130]{2,1,0:T(1,128)S(1)}, u32[]{:S(2)}, u32[]{:S(2)}) collective-permute-start(f32[1,1,130]{2,1,0:T(1,128)S(1)} %get-tuple-element.146), channel_id=1, source_target_pairs={{0,1},{1,2},{2,3},{3,0},{4,5},{5,6},{6,7},{7,4},{8,9},{9,10},{10,1... | collective-permute-start | bytes 1568 | tf_op jit(solution)/shard_map/ppermute | solution.py:25
  419.8 8.9 %collective-permute-start.131 = (f32[1,1,130]{2,1,0:T(1,128)S(1)}, f32[1,1,130]{2,1,0:T(1,128)S(1)}, u32[]{:S(2)}, u32[]{:S(2)}) collective-permute-start(f32[1,1,130]{2,1,0:T(1,128)S(1)} %get-tuple-element.145), channel_id=1, source_target_pairs={{1,0},{2,1},{3,2},{0,3},{5,4},{6,5},{7,6},{4,7},{9,8},{10,9},{11,1... | collective-permute-start | bytes 1568 | tf_op jit(solution)/shard_map/ppermute | solution.py:28
  525.2 9.0 %collective-permute-start.139 = (f32[1,1,130]{2,1,0:T(1,128)S(1)}, f32[1,1,130]{2,1,0:T(1,128)S(1)}, u32[]{:S(2)}, u32[]{:S(2)}) collective-permute-start(f32[1,1,130]{2,1,0:T(1,128)S(1)} %get-tuple-element.144), channel_id=1, source_target_pairs={{0,1},{1,2},{2,3},{3,0},{4,5},{5,6},{6,7},{7,4},{8,9},{9,10},{10,1... | collective-permute-start | bytes 1568 | tf_op jit(solution)/shard_map/ppermute | solution.py:25
  527.5 8.9 %collective-permute-start.138 = (f32[1,1,130]{2,1,0:T(1,128)S(1)}, f32[1,1,130]{2,1,0:T(1,128)S(1)}, u32[]{:S(2)}, u32[]{:S(2)}) collective-permute-start(f32[1,1,130]{2,1,0:T(1,128)S(1)} %get-tuple-element.143), channel_id=1, source_target_pairs={{1,0},{2,1},{3,2},{0,3},{5,4},{6,5},{7,6},{4,7},{9,8},{10,9},{11,1... | collective-permute-start | bytes 1568 | tf_op jit(solution)/shard_map/ppermute | solution.py:28
  633.6 9.2 %collective-permute-start.142 = (f32[1,1,130]{2,1,0:T(1,128)S(1)}, f32[1,1,130]{2,1,0:T(1,128)S(1)}, u32[]{:S(2)}, u32[]{:S(2)}) collective-permute-start(f32[1,1,130]{2,1,0:T(1,128)S(1)} %get-tuple-element.142), channel_id=1, source_target_pairs={{0,4},{4,0},{8,12},{12,8},{16,20},{20,16},{24,28},{28,24},{1,5},{5... | collective-permute-start | bytes 1568 | tf_op jit(solution)/shard_map/ppermute | solution.py:34
  639.6 8.0 %collective-permute-start.146 = (f32[1,1,130]{2,1,0:T(1,128)S(1)}, f32[1,1,130]{2,1,0:T(1,128)S(1)}, u32[]{:S(2)}, u32[]{:S(2)}) collective-permute-start(f32[1,1,130]{2,1,0:T(1,128)S(1)} %get-tuple-element.142), channel_id=1, source_target_pairs={{0,1},{1,2},{2,3},{3,0},{4,5},{5,6},{6,7},{7,4},{8,9},{9,10},{10,1... | collective-permute-start | bytes 1568 | tf_op jit(solution)/shard_map/ppermute | solution.py:25
  641.9 9.1 %collective-permute-start.145 = (f32[1,1,130]{2,1,0:T(1,128)S(1)}, f32[1,1,130]{2,1,0:T(1,128)S(1)}, u32[]{:S(2)}, u32[]{:S(2)}) collective-permute-start(f32[1,1,130]{2,1,0:T(1,128)S(1)} %get-tuple-element.141), channel_id=1, source_target_pairs={{1,0},{2,1},{3,2},{0,3},{5,4},{6,5},{7,6},{4,7},{9,8},{10,9},{11,1... | collective-permute-start | bytes 1568 | tf_op jit(solution)/shard_map/ppermute | solution.py:28
  700.6 9.1 %collective-permute-start.149 = (f32[1,1,130]{2,1,0:T(1,128)S(1)}, f32[1,1,130]{2,1,0:T(1,128)S(1)}, u32[]{:S(2)}, u32[]{:S(2)}) collective-permute-start(f32[1,1,130]{2,1,0:T(1,128)S(1)} %get-tuple-element.140), channel_id=1, source_target_pairs={{0,4},{4,0},{8,12},{12,8},{16,20},{20,16},{24,28},{28,24},{1,5},{5... | collective-permute-start | bytes 1568 | tf_op jit(solution)/shard_map/ppermute | solution.py:34
  705.8 8.9 %collective-permute-start.153 = (f32[1,1,130]{2,1,0:T(1,128)S(1)}, f32[1,1,130]{2,1,0:T(1,128)S(1)}, u32[]{:S(2)}, u32[]{:S(2)}) collective-permute-start(f32[1,1,130]{2,1,0:T(1,128)S(1)} %get-tuple-element.140), channel_id=1, source_target_pairs={{0,1},{1,2},{2,3},{3,0},{4,5},{5,6},{6,7},{7,4},{8,9},{9,10},{10,1... | collective-permute-start | bytes 1568 | tf_op jit(solution)/shard_map/ppermute | solution.py:25
  708.1 9.8 %collective-permute-start.152 = (f32[1,1,130]{2,1,0:T(1,128)S(1)}, f32[1,1,130]{2,1,0:T(1,128)S(1)}, u32[]{:S(2)}, u32[]{:S(2)}) collective-permute-start(f32[1,1,130]{2,1,0:T(1,128)S(1)} %get-tuple-element.139), channel_id=1, source_target_pairs={{1,0},{2,1},{3,2},{0,3},{5,4},{6,5},{7,6},{4,7},{9,8},{10,9},{11,1... | collective-permute-start | bytes 1568 | tf_op jit(solution)/shard_map/ppermute | solution.py:28
  (177 other events, 2141.6 us)
where the time goes:
time: 730 us; the launch traced here: 720 us
  blocking collectives  285 us (39%)
  starting transfers between devices  217 us (30%)
  waiting for transfers between devices  118 us (16%)
  other arithmetic  59.8 us (8%)
  local copies, waits for them, and re-layouts  27.7 us (4%)
  between operations  12 us (2%)
    psum x4, blocking collectives, squares(): return lax.psum(jnp.sum(residual * residual), ('lon', 'lat'))  166 us
    ppermute x44, starting transfers between devices, extended(): lax.ppermute(lax.slice_in_dim(block, 0, width, axis=dim), axis, backward)  122 us
    psum x3, blocking collectives, barotropic(): step_size = old_norm / lax.psum(jnp.sum(direction * image), ('lon', 'lat'))  119 us
    ppermute x66, waiting for transfers between devices, from_partner(): lax.ppermute(array, axis, [(i, i ^ 1 << apart) for i in range(lax.axis_si...  84.7 us
    ppermute x66, starting transfers between devices, from_partner(): lax.ppermute(array, axis, [(i, i ^ 1 << apart) for i in range(lax.axis_si...  74.8 us
    ppermute x44, waiting for transfers between devices, extended(): lax.ppermute(lax.slice_in_dim(block, block.shape[dim] - width, None, axis...  33.4 us
    ppermute x44, starting transfers between devices, extended(): lax.ppermute(lax.slice_in_dim(block, block.shape[dim] - width, None, axis...  20.4 us
  transfers between devices with their start and end apart: 154, of which 62 were waited for; matrix products, arithmetic and copies ran while one was open for 8% of the time, Pallas kernels for 0%

commit v1 on v0

v1 whole, which is shorter than its diff:
```python
import functools
import math

import jax
import jax.numpy as jnp
from jax import lax
from jax.experimental import pallas as pl
from jax.experimental.pallas import tpu as pltpu
from jax.sharding import PartitionSpec as P

SUBCYCLES = 8
SOLVE_ITERS = 4
flow_step = 0.3
slope_step = 0.3
floor_diag = 0.05

PAD = 8
DEEP = 24
MESH = pl.DeviceIdType.MESH
F32 = jnp.float32

MID = floor_diag + 9.0
HALF = 9.0


def roll(x, shift, axis):
    return pltpu.roll(x, shift % x.shape[axis], axis)


def east(x):
    return roll(x, -1, x.ndim - 1)


def west(x):
    return roll(x, 1, x.ndim - 1)


def north(x):
    return roll(x, -1, x.ndim - 2)


def south(x):
    return roll(x, 1, x.ndim - 2)


def reversal(size):
    rows = lax.broadcasted_iota(jnp.int32, (size, size), 0)
    cols = lax.broadcasted_iota(jnp.int32, (size, size), 1)
    return jnp.where(rows + cols == size - 1, 1.0, 0.0).astype(F32)


def times(a, b):
    return jnp.dot(a, b, precision=lax.Precision.HIGHEST, preferred_element_type=F32)


def kernel(
    n_lon,
    n_lat,
    tracer_ref,
    velocity_ref,
    levels_ref,
    diff_ref,
    visc_ref,
    depth_ref,
    wind_ref,
    tracer_out,
    velocity_out,
    surface_out,
    fields,
    flats,
    firsts,
    near,
    statics,
    weights,
    flow,
    height,
    row_send,
    row_recv,
    col_send,
    col_recv,
    stat_recv,
    flow_recv,
    fold_recv,
    lat_sums,
    lon_sums,
    lat_parts,
    lon_parts,
    faces,
    send_sems,
    recv_sems,
    lat_send,
    lat_recv,
    lon_send,
    lon_recv,
):
    count = tracer_ref.shape[0] // 2
    rows, cols = levels_ref.shape
    top_row = PAD + rows
    lon = lax.axis_index("lon")
    lat = lax.axis_index("lat")
    right = lax.rem(lon + 1, n_lon)
    left = lax.rem(lon + n_lon - 1, n_lon)
    mirror = n_lon - 1 - lon
    top = lat == n_lat - 1
    bottom = lat == 0
    above = jnp.minimum(lat + 1, n_lat - 1)
    below = jnp.maximum(lat - 1, 0)

    def remote(src, dst, send, recv, device):
        return pltpu.make_async_remote_copy(
            src_ref=src, dst_ref=dst, send_sem=send, recv_sem=recv, device_id=device, device_id_type=MESH
        )

    barrier = pltpu.get_barrier_semaphore()
    for apart in range(1, n_lon):
        pl.semaphore_signal(
            barrier, inc=1, device_id={"lon": lax.rem(lon + apart, n_lon)}, device_id_type=MESH
        )
    for apart in range(1, n_lat):
        pl.semaphore_signal(
            barrier, inc=1, device_id={"lat": lax.rem(lat + apart, n_lat)}, device_id_type=MESH
        )

    kinds = 4 * count + 3
    packed = -(-2 * kinds // 8) * 8
    levels_float = levels_ref[...].astype(F32)
    flats[0, PAD:top_row, :] = visc_ref[...]
    flats[1, PAD:top_row, :] = diff_ref[...]
    flats[2, PAD:top_row, :] = levels_float
    fields[0 : 2 * count, PAD:top_row, :] = velocity_ref[...]
    fields[2 * count :, PAD:top_row, :] = tracer_ref[...]

    def block_of(k):
        return (fields, k) if k < 4 * count else (flats, k - 4 * count)

    for k in range(kinds):
        ref, index = block_of(k)
        row_send[0, 2 * k : 2 * k + 2, :] = ref[index, top_row - 2 : top_row, :]
        row_send[1, 2 * k : 2 * k + 1, :] = ref[index, PAD + 1 : PAD + 2, :]
        row_send[1, 2 * k + 1 : 2 * k + 2, :] = ref[index, PAD : PAD + 1, :]
    row_send[:, 2 * kinds : packed, :] = jnp.zeros((2, packed - 2 * kinds, cols), F32)
    statics[0, DEEP : DEEP + rows, 0:cols] = depth_ref[...]
    statics[1, DEEP : DEEP + rows, 0:cols] = levels_float
    for f in range(2):
        at = packed + f * DEEP
        row_send[0, at : at + DEEP, :] = statics[f, rows : rows + DEEP, 0:cols]
        row_send[1, at : at + DEEP, :] = statics[f, DEEP : 2 * DEEP, 0:cols]

    pl.semaphore_wait(barrier, n_lon + n_lat - 2)

    def rows_out(src, dst, stage):
        @pl.when(top)
        def _():
            remote(src(0), dst(0), send_sems.at[stage, 0], recv_sems.at[stage, 0], {"lon": mirror}).start()

        @pl.when(jnp.logical_not(top))
        def _():
            remote(src(0), dst(1), send_sems.at[stage, 0], recv_sems.at[stage, 1], {"lat": above}).start()

        @pl.when(jnp.logical_not(bottom))
        def _():
            remote(src(1), dst(0), send_sems.at[stage, 1], recv_sems.at[stage, 0], {"lat": below}).start()

    def rows_in(src, dst, stage):
        remote(src(0), dst(0), send_sems.at[stage, 0], recv_sems.at[stage, 0], {"lat": above}).wait_recv()

        @pl.when(jnp.logical_not(bottom))
        def _():
            remote(src(1), dst(1), send_sems.at[stage, 1], recv_sems.at[stage, 1], {"lat": below}).wait_recv()

    def rows_sent(src, dst, stage):
        remote(src(0), dst(0), send_sems.at[stage, 0], recv_sems.at[stage, 0], {"lat": above}).wait_send()

        @pl.when(jnp.logical_not(bottom))
        def _():
            remote(src(1), dst(1), send_sems.at[stage, 1], recv_sems.at[stage, 1], {"lat": below}).wait_send()

    def cols_copies(to_east, to_west, dst, stage):
        return (
            remote(to_east, dst(0), send_sems.at[stage, 0], recv_sems.at[stage, 0], {"lon": right}),
            remote(to_west, dst(1), send_sems.at[stage, 1], recv_sems.at[stage, 1], {"lon": left}),
        )

    row_src = lambda i: row_send.at[i]
    row_dst = lambda i: row_recv.at[i]

    @pl.when(bottom)
    def _():
        row_recv[1] = jnp.zeros(row_recv.shape[1:], F32)

    rows_out(row_src, row_dst, 0)

    lane = lax.broadcasted_iota(jnp.int32, (rows, cols), 1)
    own = jnp.zeros((rows, cols), F32)
    inner = jnp.zeros((rows, cols), F32)
    for k in range(kinds):
        ref, index = block_of(k)
        x = ref[index, PAD:top_row, :]
        pair = jnp.right_shift(lane, 1) == k
        own = jnp.where(pair, roll(x, 2 * k + 1, 1), own)
        if k < 2 * count or k == kinds - 1:
            odd_part = jnp.bitwise_and(lane, 1) == 1
            inner = jnp.where(pair, jnp.where(odd_part, roll(x, 2 * k, 1), roll(x, 2 * k + 2, 1)), inner)

    rows_in(row_src, row_dst, 0)

    @pl.when(top)
    def _():
        back = reversal(cols)
        turned = times(row_recv[0], back)
        ids = lax.broadcasted_iota(jnp.int32, turned.shape, 0)
        row_recv[0] = jnp.where(ids < 4 * count, -turned, turned)
        for f in range(2):
            at = packed + f * DEEP
            row_recv[0, at : at + DEEP, :] = times(reversal(DEEP), row_recv[0, at : at + DEEP, :])

    for k in range(kinds):
        ref, index = block_of(k)
        ref[index, top_row : top_row + 1, :] = row_recv[0, 2 * k + 1 : 2 * k + 2, :]
        ref[index, top_row + 1 : top_row + 2, :] = row_recv[0, 2 * k : 2 * k + 1, :]
        ref[index, PAD - 2 : PAD, :] = row_recv[1, 2 * k : 2 * k + 2, :]
    for f in range(2):
        at = packed + f * DEEP
        statics[f, 0:DEEP, 0:cols] = row_recv[1, at : at + DEEP, :]
        statics[f, DEEP + rows :, 0:cols] = row_recv[0, at : at + DEEP, :]

    tall = rows + 2 * PAD
    lane = lax.broadcasted_iota(jnp.int32, (tall, cols), 1)
    odd = jnp.bitwise_and(lane, 1) == 1

    def corner(received):
        square = jnp.concatenate([received, jnp.zeros((cols - packed, cols), F32)], axis=0)
        turned = jnp.transpose(square)
        lane_row = lax.broadcasted_iota(jnp.int32, (1, cols), 1)
        return jnp.where(
            jnp.bitwise_and(lane_row, 1) == 1,
            turned[0:1, :],
            roll(turned[cols - PAD :, :], -1, 1)[PAD - 1 :, :],
        )

    near[0] = jnp.zeros((tall, cols), F32)
    near[1] = jnp.zeros((tall, cols), F32)
    near[0, PAD:top_row, :] = own
    near[1, PAD:top_row, :] = inner
    near[0, PAD - 1 : PAD, :] = corner(row_recv[1, 0:packed, :])
    near[0, top_row : top_row + 1, :] = corner(row_recv[0, 0:packed, :])
    own, inner = near[0], near[1]
    col_send[1] = jnp.where(odd, own, east(inner))
    col_send[0] = jnp.where(odd, west(inner), own)
    col_send[1] = jnp.where(odd, own, roll(inner, -1, 1))
    col_send[0] = jnp.where(odd, roll(inner, 1, 1), own)
    cols_dst = lambda i: col_recv.at[i]
    stat_dst = lambda i: stat_recv.at[i]
    stat_src = statics.at[:, :, 0:cols]
    col_copies = cols_copies(col_send.at[0], col_send.at[1], cols_dst, 1)
    stat_copies = cols_copies(stat_src, stat_src, stat_dst, 2)
    for copy in col_copies + stat_copies:
        copy.start()
    rows_sent(row_src, row_dst, 0)
    for copy in col_copies:
        copy.wait_recv()

    from_west, from_east = col_recv[0], col_recv[1]
    close = jnp.where(odd, roll(from_west, 1, 1), roll(from_east, -1, 1))
    far = jnp.where(odd, from_west, from_east)
    near[1] = close

    field_of = jnp.right_shift(lane, 1)
    level_of = lax.rem(field_of, count).astype(F32)

    def packed_wet(pack):
        at = 2 * (kinds - 1)
        level = jnp.where(odd, pack[:, at + 1 : at + 2], pack[:, at : at + 1])
        return jnp.where(level_of < level, 1.0, 0.0)

    wet_own, wet_close, wet_far = packed_wet(own), packed_wet(close), packed_wet(far)
    firsts[...] = wet_close * (
        wet_own * (own - close)
        + wet_far * (far - close)
        + north(wet_close) * (north(close) - close)
        + south(wet_close) * (south(close) - close)
    )

    first_lane, last_lane = lane == 0, lane == cols - 1

    def sides(x, pack, k):
        rim = pltpu.roll(pack, cols - 1 - 2 * k, 1)
        return jnp.where(last_lane, rim, east(x)), jnp.where(first_lane, rim, west(x))

    for index in range(2):
        c = flats[index]
        c_east, c_west = sides(c, close, 4 * count + index)
        for n, other in enumerate((c_east, c_west, north(c), south(c))):
            faces[index, n] = 0.5 * (c + other)
    depth_levels = flats[2]
    lev_east, lev_west = sides(depth_levels, close, kinds - 1)
    faces[2, 0] = lev_east
    faces[2, 1] = lev_west

    row_ids = (lat * rows + lax.broadcasted_iota(jnp.int32, (rows, cols), 0)).astype(F32)
    coriolis = 0.25 * jnp.sin(math.pi * ((row_ids + 0.5) / (rows * n_lat) - 0.5))

    def wet_sides(level):
        wet = jnp.where(level < flats[2], 1.0, 0.0)
        return (
            wet,
            wet * jnp.where(level < faces[2, 0], 1.0, 0.0),
            wet * jnp.where(level < faces[2, 1], 1.0, 0.0),
            wet * north(wet),
            wet * south(wet),
        )

    surface_out[...] = jnp.zeros((rows, cols), F32)
    flow[...] = jnp.zeros(flow.shape, F32)

    def velocity_level(level, carry):
        wet, w_east, w_west, w_north, w_south = wet_sides(level.astype(F32))
        coefficient = [faces[0, n] * w for n, w in enumerate((w_east, w_west, w_north, w_south))]
        wet_centre = wet[PAD:top_row]
        pair = []
        for comp in range(2):
            k = comp * count + level
            x = fields[k]
            x_east, x_west = sides(x, near[1], k)
            first = (
                w_east * (x_east - x)
                + w_west * (x_west - x)
                + w_north * (north(x) - x)
                + w_south * (south(x) - x)
            )
            f_east, f_west = sides(first, firsts[...], k)
            second = (
                coefficient[0] * (f_east - first)
                + coefficient[1] * (f_west - first)
                + coefficient[2] * (north(first) - first)
                + coefficient[3] * (south(first) - first)
            )
            pair.append((x[PAD:top_row], second[PAD:top_row]))
        (u, lap_u), (v, lap_v) = pair
        star_u = wet_centre * (u - lap_u + coriolis * v)
        star_v = wet_centre * (v - lap_v - coriolis * u)
        velocity_out[level] = star_u
        velocity_out[count + level] = star_v
        flow[0, DEEP : DEEP + rows, 0:cols] += star_u
        flow[1, DEEP : DEEP + rows, 0:cols] += star_v
        return carry

    lax.fori_loop(0, count, velocity_level, 0)

    levels_here = flats[2, PAD:top_row, :]
    ocean_here = jnp.where(levels_here > 0, 1.0, 0.0)
    for comp in range(2):
        mean = flow[comp, DEEP : DEEP + rows, 0:cols] / jnp.maximum(levels_here, 1.0)
        height[1 + comp, 0:rows, 0:cols] = mean
        flow[comp, DEEP : DEEP + rows, 0:cols] = mean + wind_ref[comp] * ocean_here

    flow_edge = lambda i: flow.at[:, rows : rows + DEEP, 0:cols] if i == 0 else flow.at[:, DEEP : 2 * DEEP, 0:cols]
    fold_dst = lambda i: fold_recv.at[i]
    rows_out(flow_edge, fold_dst, 3)

    def tracer_level(level, carry):
        _, w_east, w_west, w_north, w_south = wet_sides(level.astype(F32))
        coefficient = [faces[1, n] * w for n, w in enumerate((w_east, w_west, w_north, w_south))]
        for comp in range(2):
            k = comp * count + level
            x = fields[2 * count + k]
            x_east, x_west = sides(x, near[1], 2 * count + k)
            change = (
                coefficient[0] * (x_east - x)
                + coefficient[1] * (x_west - x)
                + coefficient[2] * (north(x) - x)
                + coefficient[3] * (south(x) - x)
            )
            tracer_out[k] = (x + change)[PAD:top_row]
        return carry

    lax.fori_loop(0, count // 2, tracer_level, 0)

    rows_in(flow_edge, fold_dst, 3)

    @pl.when(top)
    def _():
        for comp in range(2):
            turned = times(fold_recv[0, comp], reversal(cols))
            fold_recv[0, comp] = -times(reversal(DEEP), turned)

    for comp in range(2):
        flow[comp, DEEP + rows :, 0:cols] = fold_recv[0, comp]

    @pl.when(jnp.logical_not(bottom))
    def _():
        for comp in range(2):
            flow[comp, 0:DEEP, 0:cols] = fold_recv[1, comp]

    flow_src = flow.at[:, :, 0:cols]
    flow_dst = lambda i: flow_recv.at[i]
    flow_copies = cols_copies(flow_src, flow_src, flow_dst, 4)
    for copy in flow_copies:
        copy.start()
    lax.fori_loop(count // 2, count, tracer_level, 0)
    rows_sent(flow_edge, fold_dst, 3)

    for copy in stat_copies:
        copy.wait_recv()
    deep_rows = rows + 2 * DEEP
    half = lax.broadcasted_iota(jnp.int32, (deep_rows, cols), 1) < cols // 2
    for f in range(2):
        statics[f, :, cols:] = jnp.where(half, stat_recv[1, f], stat_recv[0, f])
    depth = statics[0]
    ocean = jnp.where(statics[1] > 0, 1.0, 0.0)
    ocean_ref = weights.at[9]
    ocean_ref[...] = ocean
    total = floor_diag * ocean + (1.0 - ocean)
    shifts = []
    for move in (lambda x: x, north, south):
        d, o = move(depth), move(ocean)
        if move in (north, south):
            shifts.append((1.0, d, o))
        scale = 0.5 if move in (north, south) else 1.0
        shifts.append((scale, east(d), east(o)))
        shifts.append((scale, west(d), west(o)))
    for n, (scale, d, o) in enumerate(shifts):
        weight = scale * 0.5 * (depth + d) * ocean * o
        weights[n] = weight
        total = total + weight
    weights[8] = total

    for copy in flow_copies:
        copy.wait_recv()
    for copy in flow_copies:
        copy.wait_send()
    for comp in range(2):
        flow[comp, :, cols:] = jnp.where(half, flow_recv[1, comp], flow_recv[0, comp])

    height[0] = jnp.zeros(height.shape[1:], F32)

    def subcycle(step, carry):
        flux_east = statics[0] * flow[0]
        flux_north = statics[0] * flow[1]
        ocean_now = weights[9]
        divergence = (east(flux_east) - west(flux_east)) + (north(flux_north) - south(flux_north))
        high = height[0] - (0.5 * flow_step) * ocean_now * divergence
        height[0] = high
        flow[0] = flow[0] - (0.5 * slope_step) * ocean_now * (east(high) - west(high))
        flow[1] = flow[1] - (0.5 * slope_step) * ocean_now * (north(high) - south(high))
        return carry

    lax.fori_loop(0, SUBCYCLES, subcycle, 0)

    def operate(p):
        up, down = north(p), south(p)
        summed = weights[8] * p - weights[0] * east(p) - weights[1] * west(p)
        summed = summed - weights[2] * up - weights[3] * east(up) - weights[4] * west(up)
        return summed - weights[5] * down - weights[6] * east(down) - weights[7] * west(down)

    basis = [height[0]]
    for n in range(SOLVE_ITERS):
        v = basis[-1]
        scaled = (operate(v) - MID * v) * ((1.0 if n == 0 else 2.0) / HALF)
        basis.append(scaled if n == 0 else scaled - basis[-2])

    pairs = [(i, j) for i in range(SOLVE_ITERS) for j in range(i, SOLVE_ITERS + 1)]
    inside = [v[DEEP : DEEP + rows, 0:cols] for v in basis]
    lat_parts[...] = jnp.zeros(lat_parts.shape, F32)
    for n, (i, j) in enumerate(pairs):
        lat_parts[n : n + 1, :] = jnp.sum(inside[i] * inside[j], axis=0, keepdims=True)

    def all_sum(parts, slots, sends, recvs, axis, me, size):
        copies = [
            remote(parts, slots.at[d - 1], sends.at[d - 1], recvs.at[d - 1], {axis: lax.rem(me + d, size)})
            for d in range(1, size)
        ]
        for copy in copies:
            copy.start()
        for copy in copies:
            copy.wait()
        result = parts[...]
        for d in range(1, size):
            result = result + slots[d - 1]
        return result

    lon_parts[...] = all_sum(lat_parts, lat_sums, lat_send, lat_recv, "lat", lat, n_lat)
    sums = jnp.sum(
        all_sum(lon_parts, lon_sums, lon_send, lon_recv, "lon", lon, n_lon), axis=1, keepdims=True
    )
    gram = {}
    for n, (i, j) in enumerate(pairs):
        gram[i, j] = gram[j, i] = sums[n : n + 1, :]

    def inner_product(a, b):
        result = None
        for i, x in a.items():
            for j, y in b.items():
                term = x * y * gram[i, j]
                result = term if result is None else result + term
        return result

    def image_of(a):
        result = {}

        def add(n, value):
            result[n] = result[n] + value if n in result else value

        for n, x in a.items():
            add(n, MID * x)
            add(n + 1, (HALF if n == 0 else 0.5 * HALF) * x)
            if n > 0:
                add(n - 1, 0.5 * HALF * x)
        return result

    one = jnp.ones((1, 1), F32)
    residual = {0: one}
    direction = {0: one}
    answer = {}
    norm = inner_product(residual, residual)
    for iteration in range(SOLVE_ITERS):
        image = image_of(direction)
        step = norm / inner_product(direction, image)
        for n, x in direction.items():
            answer[n] = answer[n] + step * x if n in answer else step * x
        if iteration < SOLVE_ITERS - 1:
            residual = {n: (residual[n] if n in residual else 0.0) - step * x for n, x in image.items()}
            new_norm = inner_product(residual, residual)
            ratio = new_norm / norm
            direction = {
                n: x + ratio * direction[n] if n in direction else x for n, x in residual.items()
            }
            norm = new_norm
    surface = None
    for n, x in answer.items():
        term = x * basis[n]
        surface = term if surface is None else surface + term
    surface_out[...] = surface[DEEP : DEEP + rows, 0:cols]

    slopes = (east(surface) - west(surface), north(surface) - south(surface))
    for comp, slope in enumerate(slopes):
        final = flow[comp] - (0.5 * slope_step) * weights[9] * slope
        height[1 + comp, 0:rows, 0:cols] = final[DEEP : DEEP + rows, 0:cols] - height[1 + comp, 0:rows, 0:cols]

    def correct(level, carry):
        wet = level.astype(F32) < flats[2, PAD:top_row, :]
        for comp in range(2):
            k = comp * count + level
            velocity_out[k] = velocity_out[k] + jnp.where(wet, height[1 + comp, 0:rows, 0:cols], 0.0)
        return carry

    lax.fori_loop(0, count, correct, 0)
    for copy in col_copies + stat_copies:
        copy.wait_send()


def per_device(n_lon, n_lat, tracers, velocity, active_levels, diffusivity, viscosity, ocean_depth, wind_forcing):
    _, count, rows, cols = tracers.shape
    kinds = 4 * count + 3
    packed = -(-2 * kinds // 8) * 8
    message = packed + 2 * DEEP
    tall, deep_rows = rows + 2 * PAD, rows + 2 * DEEP
    entries = 16
    block = jax.ShapeDtypeStruct((2 * count, rows, cols), F32)
    vmem = pl.BlockSpec(memory_space=pltpu.VMEM)
    out = pl.pallas_call(
        functools.partial(kernel, n_lon, n_lat),
        out_shape=(block, block, jax.ShapeDtypeStruct((rows, cols), F32)),
        in_specs=[vmem] * 7,
        out_specs=(vmem, vmem, vmem),
        scratch_shapes=[
            pltpu.VMEM((4 * count, tall, cols), F32),
            pltpu.VMEM((3, tall, cols), F32),
            pltpu.VMEM((tall, cols), F32),
            pltpu.VMEM((2, tall, cols), F32),
            pltpu.VMEM((2, deep_rows, 2 * cols), F32),
            pltpu.VMEM((10, deep_rows, 2 * cols), F32),
            pltpu.VMEM((2, deep_rows, 2 * cols), F32),
            pltpu.VMEM((3, deep_rows, 2 * cols), F32),
            pltpu.VMEM((2, message, cols), F32),
            pltpu.VMEM((2, message, cols), F32),
            pltpu.VMEM((2, tall, cols), F32),
            pltpu.VMEM((2, tall, cols), F32),
            pltpu.VMEM((2, 2, deep_rows, cols), F32),
            pltpu.VMEM((2, 2, deep_rows, cols), F32),
            pltpu.VMEM((2, 2, DEEP, cols), F32),
            pltpu.VMEM((n_lat - 1, entries, cols), F32),
            pltpu.VMEM((n_lon - 1, entries, cols), F32),
            pltpu.VMEM((entries, cols), F32),
            pltpu.VMEM((entries, cols), F32),
            pltpu.VMEM((3, 4, tall, cols), F32),
            pltpu.SemaphoreType.DMA((5, 2)),
            pltpu.SemaphoreType.DMA((5, 2)),
            pltpu.SemaphoreType.DMA((n_lat - 1,)),
            pltpu.SemaphoreType.DMA((n_lat - 1,)),
            pltpu.SemaphoreType.DMA((n_lon - 1,)),
            pltpu.SemaphoreType.DMA((n_lon - 1,)),
        ],
        compiler_params=pltpu.CompilerParams(
            collective_id=0, has_side_effects=True, vmem_limit_bytes=40 * 1024 * 1024
        ),
    )(
        tracers.reshape(2 * count, rows, cols),
        velocity.reshape(2 * count, rows, cols),
        active_levels,
        diffusivity,
        viscosity,
        ocean_depth,
        wind_forcing,
    )
    return out[0].reshape(tracers.shape), out[1].reshape(velocity.shape), out[2]


def solution(mesh):
    flat = P("lat", "lon")
    deep = P(None, None, "lat", "lon")
    return jax.shard_map(
        functools.partial(per_device, mesh.shape["lon"], mesh.shape["lat"]),
        mesh=mesh,
        in_specs=(deep, deep, flat, flat, flat, flat, P(None, "lat", "lon")),
        out_specs=(deep, deep, flat),
        check_vma=False,
    )
```

time: 730 us -> 44.2 us (0.06); the launches traced: 720 us -> 43.7 us
  blocking collectives: 285 us -> 0 us
  starting transfers between devices: 217 us -> 0 us
  waiting for transfers between devices: 118 us -> 0 us
  other arithmetic: 59.8 us -> 0 us
  Pallas kernels: 0 us -> 34.7 us
  local copies, waits for them, and re-layouts: 27.7 us -> 8.32 us
  between operations: 12 us -> 0.66 us
    psum x7 -> x0, blocking collectives: 285 us -> none  [the longest x4 166 us: squares(): return lax.psum(jnp.sum(residual * residual), ('lon', 'lat'))]
    ppermute x154 -> x0, starting transfers between devices: 217 us -> none  [the longest x44 122 us: extended(): lax.ppermute(lax.slice_in_dim(block, 0, width, axis=dim), axis, backward)]
    ppermute x154 -> x0, waiting for transfers between devices: 118 us -> none  [the longest x66 84.7 us: from_partner(): lax.ppermute(array, axis, [(i, i ^ 1 << apart) for i in range(lax.axis_si...]
    pallas_call x0 -> x1, Pallas kernels: none -> 34.7 us  [per_device(): pl.pallas_call(functools.partial(kernel, n_lon, n_lat), out_shape=(block,...]
    slice x35 -> x0, local copies, waits for them, and re-layouts: 16.6 us -> none  [the longest x5 9.67 us: window(): lax.slice_in_dim(inner, 1 + col_off, 1 + col_off + col_count, axis=field....]
    slice x40 -> x0, other arithmetic: 15.6 us -> none  [the longest x27 9.55 us: window(): lax.slice_in_dim(field, 1 + row_off, 1 + row_off + row_count, axis=field....]
    reduce_sum x8 -> x0, other arithmetic: 13.8 us -> none  [the longest x4 8.15 us: barotropic(): step_size = old_norm / lax.psum(jnp.sum(direction * image), ('lon', 'lat'))]
    add x8 -> x0, other arithmetic: 9.2 us -> none  [the longest x1 5.09 us: per_device(): tracers_out = tracers + tracer_lap]
  transfers between devices with their start and end apart: 154 -> 0, of which waited for: 62 -> 0; matrix products, arithmetic and copies ran while one was open for 8% -> 0% of each run, Pallas kernels for 0% -> 0%
where the time goes in v1:
time: 44.2 us; the launch traced here: 43.7 us
  Pallas kernels  34.7 us (79%)
  local copies, waits for them, and re-layouts  8.32 us (19%)
  between operations  0.66 us (1%)
    pallas_call x1, Pallas kernels, per_device(): pl.pallas_call(functools.partial(kernel, n_lon, n_lat), out_shape=(block,...  34.7 us
    unnamed x17, local copies, waits for them, and re-layouts  8.32 us

profile of v1, /device:TPU:0, one launch (start us, length us, event | category | flops | bytes accessed | tf_op | source)
XLA Modules:
  0.0 43.7 jit_solution(16474683555954261517)
XLA Ops:
  0.6 0.0 copy-start
  0.6 1.1 %copy-done = f32[2,10,64,128]{3,2,1,0:T(8,128)S(1)} copy-done((f32[2,10,64,128]{3,2,1,0:T(8,128)S(1)}, f32[2,10,64,128]{3,2,1,0:T(8,128)}, u32[]{:S(2)}) %copy-start) | copy-done | bytes 655384
  1.7 0.0 copy-start.1
  1.7 1.1 %copy-done.1 = f32[2,10,64,128]{3,2,1,0:T(8,128)S(1)} copy-done((f32[2,10,64,128]{3,2,1,0:T(8,128)S(1)}, f32[2,10,64,128]{3,2,1,0:T(8,128)}, u32[]{:S(2)}) %copy-start.1) | copy-done | bytes 655384
  2.8 0.0 copy-start.2
  2.8 0.8 %copy-done.2 = f32[2,64,128]{2,1,0:T(8,128)S(1)} copy-done((f32[2,64,128]{2,1,0:T(8,128)S(1)}, f32[2,64,128]{2,1,0:T(8,128)}, u32[]{:S(2)}) %copy-start.2) | copy-done | bytes 65560
  3.6 0.0 copy-start.3
  3.7 0.8 %copy-done.3 = s32[64,128]{1,0:T(8,128)S(1)} copy-done((s32[64,128]{1,0:T(8,128)S(1)}, s32[64,128]{1,0:T(8,128)}, u32[]{:S(2)}) %copy-start.3) | copy-done | bytes 32792
  4.4 0.0 copy-start.4
  4.4 0.8 %copy-done.4 = f32[64,128]{1,0:T(8,128)S(1)} copy-done((f32[64,128]{1,0:T(8,128)S(1)}, f32[64,128]{1,0:T(8,128)}, u32[]{:S(2)}) %copy-start.4) | copy-done | bytes 32792
  5.2 0.0 copy-start.5
  5.2 0.8 %copy-done.5 = f32[64,128]{1,0:T(8,128)S(1)} copy-done((f32[64,128]{1,0:T(8,128)S(1)}, f32[64,128]{1,0:T(8,128)}, u32[]{:S(2)}) %copy-start.5) | copy-done | bytes 32792
  5.9 0.0 copy-start.6
  5.9 0.8 %copy-done.6 = f32[64,128]{1,0:T(8,128)S(1)} copy-done((f32[64,128]{1,0:T(8,128)S(1)}, f32[64,128]{1,0:T(8,128)}, u32[]{:S(2)}) %copy-start.6) | copy-done | bytes 32792
  6.7 34.7 %shard_map.94 = (f32[20,64,128]{2,1,0:T(8,128)S(1)}, f32[20,64,128]{2,1,0:T(8,128)S(1)}, f32[64,128]{1,0:T(8,128)S(1)}) custom-call(f32[20,64,128]{2,1,0:T(8,128)S(1)} %bitcast.4, f32[20,64,128]{2,1,0:T(8,128)S(1)} %bitcast.5, s32[64,128]{1,0:T(8,128)S(1)} %copy-done.3, f32[64,128]{1,0:T(8,128)S(1)} %copy-done.4, f32[64,128]{1,0:T(8,128)S(1)} %copy-done.5, ...), custom_call_target="tpu_custom_call" | custom-call | tf_op jit(solution)/shard_map/pallas_call | solution.py:561
  41.4 0.8 %copy.13 = f32[2,10,64,128]{3,2,1,0:T(8,128)} copy(f32[2,10,64,128]{3,2,1,0:T(8,128)S(1)} %bitcast.7) | data formatting | bytes 1310720
  42.3 0.8 %copy.14 = f32[2,10,64,128]{3,2,1,0:T(8,128)} copy(f32[2,10,64,128]{3,2,1,0:T(8,128)S(1)} %bitcast.6) | data formatting | bytes 1310720
  43.1 0.6 %copy.15 = f32[64,128]{1,0:T(8,128)} copy(f32[64,128]{1,0:T(8,128)S(1)} %get-tuple-element.14) | data formatting | bytes 65536
Async XLA Ops:
  0.6 1.1 %copy-start = (f32[2,10,64,128]{3,2,1,0:T(8,128)S(1)}, f32[2,10,64,128]{3,2,1,0:T(8,128)}, u32[]{:S(2)}) copy-start(f32[2,10,64,128]{3,2,1,0:T(8,128)} %param.7) | copy-start | bytes 1966084
  1.7 1.1 %copy-start.1 = (f32[2,10,64,128]{3,2,1,0:T(8,128)S(1)}, f32[2,10,64,128]{3,2,1,0:T(8,128)}, u32[]{:S(2)}) copy-start(f32[2,10,64,128]{3,2,1,0:T(8,128)} %param.8) | copy-start | bytes 1966084
  2.8 0.8 %copy-start.2 = (f32[2,64,128]{2,1,0:T(8,128)S(1)}, f32[2,64,128]{2,1,0:T(8,128)}, u32[]{:S(2)}) copy-start(f32[2,64,128]{2,1,0:T(8,128)} %wind_ref.1) | copy-start | bytes 196612
  3.6 0.8 %copy-start.3 = (s32[64,128]{1,0:T(8,128)S(1)}, s32[64,128]{1,0:T(8,128)}, u32[]{:S(2)}) copy-start(s32[64,128]{1,0:T(8,128)} %levels_ref.1) | copy-start | bytes 98308
  4.4 0.8 %copy-start.4 = (f32[64,128]{1,0:T(8,128)S(1)}, f32[64,128]{1,0:T(8,128)}, u32[]{:S(2)}) copy-start(f32[64,128]{1,0:T(8,128)} %diff_ref.1) | copy-start | bytes 98308
  5.2 0.8 %copy-start.5 = (f32[64,128]{1,0:T(8,128)S(1)}, f32[64,128]{1,0:T(8,128)}, u32[]{:S(2)}) copy-start(f32[64,128]{1,0:T(8,128)} %visc_ref.1) | copy-start | bytes 98308
  5.9 0.8 %copy-start.6 = (f32[64,128]{1,0:T(8,128)S(1)}, f32[64,128]{1,0:T(8,128)}, u32[]{:S(2)}) copy-start(f32[64,128]{1,0:T(8,128)} %depth_ref.1) | copy-start | bytes 98308

commit v2 on v1

v2 whole, which is shorter than its diff:
```python
import functools
import math

import jax
import jax.numpy as jnp
from jax import lax
from jax.experimental import pallas as pl
from jax.experimental.pallas import tpu as pltpu
from jax.sharding import PartitionSpec as P

SUBCYCLES = 8
SOLVE_ITERS = 4
flow_step = 0.3
slope_step = 0.3
floor_diag = 0.05

PAD = 8
DEEP = 24
STRIP = 32
MESH = pl.DeviceIdType.MESH
F32 = jnp.float32

SHIFTS = (0.0, 5.0, 2.5, 8.0)
SCALE = 5.0


def roll(x, shift, axis):
    return pltpu.roll(x, shift % x.shape[axis], axis)


def lanes(shape):
    return lax.broadcasted_iota(jnp.int32, shape, len(shape) - 1)


def lane_sides(a, b):
    cols = a.shape[-1]
    lane = lanes(a.shape)
    last, first = lane == cols - 1, lane == 0
    a_up, b_up = roll(a, -1, 1), roll(b, -1, 1)
    a_down, b_down = roll(a, 1, 1), roll(b, 1, 1)
    east = (jnp.where(last, b_up, a_up), jnp.where(last, a_up, b_up))
    west = (jnp.where(first, b_down, a_down), jnp.where(first, a_down, b_down))
    return east, west


def mirrored(x):
    return jnp.take_along_axis(x, x.shape[1] - 1 - lanes(x.shape), axis=1)


def kernel(
    n_lon,
    n_lat,
    tracer_hbm,
    velocity_hbm,
    levels_hbm,
    diff_hbm,
    visc_hbm,
    depth_hbm,
    wind_hbm,
    tracer_out,
    star_out,
    extra_out,
    fields,
    flats,
    levels_in,
    wind,
    near,
    firsts,
    laps,
    faces,
    deep,
    ocean,
    weights,
    flux,
    basis,
    row_send,
    row_recv,
    col_send,
    col_recv,
    strip_send,
    strip_recv,
    fold_recv,
    lat_sums,
    lon_sums,
    lat_parts,
    lon_parts,
    load_sems,
    send_sems,
    recv_sems,
    lat_send,
    lat_recv,
    lon_send,
    lon_recv,
):
    count = tracer_hbm.shape[0] // 2
    rows, cols = levels_hbm.shape
    top_row = PAD + rows
    deep_rows = rows + 2 * DEEP
    start = PAD + DEEP
    stop = start + rows
    end = PAD + deep_rows
    lon = lax.axis_index("lon")
    lat = lax.axis_index("lat")
    right = lax.rem(lon + 1, n_lon)
    left = lax.rem(lon + n_lon - 1, n_lon)
    mirror = n_lon - 1 - lon
    top = lat == n_lat - 1
    bottom = lat == 0
    above = jnp.minimum(lat + 1, n_lat - 1)
    below = jnp.maximum(lat - 1, 0)

    loads = [
        pltpu.make_async_copy(src, dst, load_sems.at[n])
        for n, (src, dst) in enumerate(
            (
                (velocity_hbm, fields.at[0 : 2 * count, PAD:top_row, :]),
                (tracer_hbm, fields.at[2 * count : 4 * count, PAD:top_row, :]),
                (levels_hbm, levels_in),
                (visc_hbm, flats.at[0, PAD:top_row, :]),
                (diff_hbm, flats.at[1, PAD:top_row, :]),
                (depth_hbm, deep.at[0, 0, start:stop, :]),
                (wind_hbm, wind),
            )
        )
    ]
    for load in loads:
        load.start()

    def remote(src, dst, send, recv, device):
        return pltpu.make_async_remote_copy(
            src_ref=src, dst_ref=dst, send_sem=send, recv_sem=recv, device_id=device, device_id_type=MESH
        )

    barrier = pltpu.get_barrier_semaphore()
    for apart in range(1, n_lon):
        pl.semaphore_signal(
            barrier, inc=1, device_id={"lon": lax.rem(lon + apart, n_lon)}, device_id_type=MESH
        )
    for apart in range(1, n_lat):
        pl.semaphore_signal(
            barrier, inc=1, device_id={"lat": lax.rem(lat + apart, n_lat)}, device_id_type=MESH
        )

    kinds = 4 * count + 3
    packed = -(-2 * kinds // 8) * 8
    row_send[:, 2 * kinds : packed, :] = jnp.zeros((2, packed - 2 * kinds, cols), F32)
    deep[2:4] = jnp.zeros((2,) + deep.shape[1:], F32)
    for array in (flux, ocean):
        array[:, 0:PAD, :] = jnp.zeros((2, PAD, cols), F32)
        array[:, end:, :] = jnp.zeros((2, PAD, cols), F32)
    for array in (basis, deep.at[0:2]):
        array[:, :, 0:PAD, :] = jnp.zeros((array.shape[0], 2, PAD, cols), F32)
        array[:, :, end:, :] = jnp.zeros((array.shape[0], 2, PAD, cols), F32)
    basis[0, :, PAD:end, :] = jnp.zeros((2, deep_rows, cols), F32)
    laps[...] = jnp.zeros(laps.shape, F32)
    for n in range(2):
        near[n] = jnp.zeros(near.shape[1:], F32)

    @pl.when(bottom)
    def _():
        row_recv[1] = jnp.zeros(row_recv.shape[1:], F32)

    for load in loads:
        load.wait()

    levels_float = levels_in[...].astype(F32)
    flats[2, PAD:top_row, :] = levels_float
    deep[1, 0, start:stop, :] = levels_float

    def block_of(k):
        return (fields, k) if k < 4 * count else (flats, k - 4 * count)

    for k in range(kinds):
        ref, index = block_of(k)
        row_send[0, 2 * k : 2 * k + 2, :] = ref[index, top_row - 2 : top_row, :]
        row_send[1, 2 * k : 2 * k + 1, :] = ref[index, PAD + 1 : PAD + 2, :]
        row_send[1, 2 * k + 1 : 2 * k + 2, :] = ref[index, PAD : PAD + 1, :]
    for f in range(2):
        at = packed + f * DEEP
        row_send[0, at : at + DEEP, :] = deep[f, 0, stop - DEEP : stop, :]
        row_send[1, at : at + DEEP, :] = deep[f, 0, start : start + DEEP, :]

    pl.semaphore_wait(barrier, n_lon + n_lat - 2)

    def rows_out(src, dst, stage):
        @pl.when(top)
        def _():
            remote(src(0), dst(0), send_sems.at[stage, 0], recv_sems.at[stage, 0], {"lon": mirror}).start()

        @pl.when(jnp.logical_not(top))
        def _():
            remote(src(0), dst(1), send_sems.at[stage, 0], recv_sems.at[stage, 1], {"lat": above}).start()

        @pl.when(jnp.logical_not(bottom))
        def _():
            remote(src(1), dst(0), send_sems.at[stage, 1], recv_sems.at[stage, 0], {"lat": below}).start()

    def rows_in(src, dst, stage):
        remote(src(0), dst(0), send_sems.at[stage, 0], recv_sems.at[stage, 0], {"lat": above}).wait_recv()

        @pl.when(jnp.logical_not(bottom))
        def _():
            remote(src(1), dst(1), send_sems.at[stage, 1], recv_sems.at[stage, 1], {"lat": below}).wait_recv()

    def rows_sent(src, dst, stage):
        remote(src(0), dst(0), send_sems.at[stage, 0], recv_sems.at[stage, 0], {"lat": above}).wait_send()

        @pl.when(jnp.logical_not(bottom))
        def _():
            remote(src(1), dst(1), send_sems.at[stage, 1], recv_sems.at[stage, 1], {"lat": below}).wait_send()

    def cols_copies(send, recv, stage):
        return (
            remote(send.at[0], recv.at[0], send_sems.at[stage, 0], recv_sems.at[stage, 0], {"lon": right}),
            remote(send.at[1], recv.at[1], send_sems.at[stage, 1], recv_sems.at[stage, 1], {"lon": left}),
        )

    row_src = lambda i: row_send.at[i]
    row_dst = lambda i: row_recv.at[i]
    rows_out(row_src, row_dst, 0)

    lane = lanes((rows, cols))
    own = jnp.zeros((rows, cols), F32)
    inner = jnp.zeros((rows, cols), F32)
    odd_here = jnp.bitwise_and(lane, 1) == 1
    for k in range(kinds):
        ref, index = block_of(k)
        x = ref[index, PAD:top_row, :]
        pair = jnp.right_shift(lane, 1) == k
        own = jnp.where(pair, roll(x, 2 * k + 1, 1), own)
        if k < 2 * count or k == kinds - 1:
            inner = jnp.where(pair, jnp.where(odd_here, roll(x, 2 * k, 1), roll(x, 2 * k + 2, 1)), inner)
    near[0, PAD:top_row, :] = own
    near[1, PAD:top_row, :] = inner

    rows_in(row_src, row_dst, 0)

    @pl.when(top)
    def _():
        turned = mirrored(row_recv[0])
        ids = lax.broadcasted_iota(jnp.int32, turned.shape, 0)
        turned = jnp.where(ids < 4 * count, -turned, turned)
        row_recv[0, 0:packed, :] = turned[0:packed]
        for f in range(2):
            at = packed + f * DEEP
            for n in range(DEEP):
                row_recv[0, at + n : at + n + 1, :] = turned[at + DEEP - 1 - n : at + DEEP - n]

    for f in range(2):
        at = packed + f * DEEP
        deep[f, 0, PAD:start, :] = row_recv[1, at : at + DEEP, :]
        deep[f, 0, stop:end, :] = row_recv[0, at : at + DEEP, :]

    tall = rows + 2 * PAD
    lane = lanes((tall, cols))
    odd = jnp.bitwise_and(lane, 1) == 1

    def corner(received):
        square = jnp.concatenate([received, jnp.zeros((cols - packed, cols), F32)], axis=0)
        turned = jnp.transpose(square)
        return jnp.where(
            jnp.bitwise_and(lanes((1, cols)), 1) == 1,
            turned[0:1, :],
            roll(turned[cols - PAD :, :], -1, 1)[PAD - 1 :, :],
        )

    near[0, PAD - 1 : PAD, :] = corner(row_recv[1, 0:packed, :])
    near[0, top_row : top_row + 1, :] = corner(row_recv[0, 0:packed, :])
    own, inner = near[0], near[1]
    col_send[1] = jnp.where(odd, own, roll(inner, -1, 1))
    col_send[0] = jnp.where(odd, roll(inner, 1, 1), own)
    col_copies = cols_copies(col_send, col_recv, 1)
    for copy in col_copies:
        copy.start()

    groups = cols // STRIP
    tiles = deep_rows // 8
    group_of = lanes((8, cols)) // STRIP

    def pack_strips(pair, f):
        for side, base in ((0, cols - STRIP), (1, 0)):
            for t in range(0, tiles, groups):
                strip = None
                for g in range(min(groups, tiles - t)):
                    at = PAD + 8 * (t + g)
                    x = roll(deep[2 * pair + f, 0, at : at + 8, :], STRIP * g - base, 1)
                    strip = x if strip is None else jnp.where(group_of == g, x, strip)
                strip_send[pair, side, f, 8 * (t // groups) : 8 * (t // groups) + 8, :] = strip

    def unpack_strips(pair, f):
        for j in range(tiles):
            at, t, g = PAD + 8 * j, 8 * (j // groups), j % groups
            low = roll(strip_recv[pair, 1, f, t : t + 8, :], -STRIP * g, 1)
            high = roll(strip_recv[pair, 0, f, t : t + 8, :], cols - STRIP - STRIP * g, 1)
            deep[2 * pair + f, 1, at : at + 8, :] = jnp.where(group_of < groups // 2, low, high)

    for f in range(2):
        pack_strips(0, f)
    stat_copies = cols_copies(strip_send.at[0], strip_recv.at[0], 2)
    for copy in stat_copies:
        copy.start()

    for k in range(kinds):
        ref, index = block_of(k)
        ref[index, top_row : top_row + 1, :] = row_recv[0, 2 * k + 1 : 2 * k + 2, :]
        ref[index, top_row + 1 : top_row + 2, :] = row_recv[0, 2 * k : 2 * k + 1, :]
        ref[index, PAD - 2 : PAD, :] = row_recv[1, 2 * k : 2 * k + 2, :]

    row_ids = (lat * rows + lax.broadcasted_iota(jnp.int32, (rows, cols), 0)).astype(F32)
    coriolis = 0.25 * jnp.sin(math.pi * ((row_ids + 0.5) / (rows * n_lat) - 0.5))
    faces[2, 2, 0:rows, :] = coriolis

    for copy in col_copies:
        copy.wait_recv()
    from_west, from_east = col_recv[0], col_recv[1]
    close = jnp.where(odd, roll(from_west, 1, 1), roll(from_east, -1, 1))
    far = jnp.where(odd, from_west, from_east)
    near[1] = close

    level_of = lax.rem(jnp.right_shift(lane, 1), count).astype(F32)

    def packed_wet(pack):
        at = 2 * (kinds - 1)
        level = jnp.where(odd, pack[:, at + 1 : at + 2], pack[:, at : at + 1])
        return jnp.where(level_of < level, 1.0, 0.0)

    wet_own, wet_close, wet_far = packed_wet(own), packed_wet(close), packed_wet(far)
    firsts[...] = wet_close * (
        wet_own * (own - close)
        + wet_far * (far - close)
        + roll(wet_close, -1, 0) * (roll(close, -1, 0) - close)
        + roll(wet_close, 1, 0) * (roll(close, 1, 0) - close)
    )

    def sides(x, pack, k):
        rim = pltpu.roll(pack, cols - 1 - 2 * k, 1)
        lane = lanes(x.shape)
        return (
            jnp.where(lane == cols - 1, rim, roll(x, -1, 1)),
            jnp.where(lane == 0, rim, roll(x, 1, 1)),
        )

    whole = slice(PAD, top_row)
    northern = slice(PAD + 1, top_row + 1)
    southern = slice(PAD - 1, top_row - 1)
    for index in range(2):
        c = flats[index, whole, :]
        c_east, c_west = sides(c, near[1, whole, :], 4 * count + index)
        others = (c_east, c_west, flats[index, northern, :], flats[index, southern, :])
        for n, other in enumerate(others):
            faces[index, n, 0:rows, :] = 0.5 * (c + other)
    lev_east, lev_west = sides(flats[2], near[1], kinds - 1)
    faces[2, 0] = lev_east
    faces[2, 1] = lev_west

    wide = slice(PAD - 1, top_row + PAD - 1)
    wide_north = slice(PAD, top_row + PAD)
    wide_south = slice(PAD - 2, top_row + PAD - 2)

    def masks(level, here, north, south):
        return (
            level < flats[2, here, :],
            level < faces[2, 0, here, :],
            level < faces[2, 1, here, :],
            level < flats[2, north, :],
            level < flats[2, south, :],
        )

    def weighted(x, neighbours, wets, index):
        total = None
        for n, other in enumerate(neighbours):
            term = faces[index, n, 0:rows, :] * jnp.where(wets[n + 1], other - x, 0.0)
            total = term if total is None else total + term
        return total

    def velocity_level(level, carry):
        level_float = level.astype(F32)
        wets = masks(level_float, wide, wide_north, wide_south)
        for comp in range(2):
            k = comp * count + level
            x = fields[k, wide, :]
            x_east, x_west = sides(x, near[1, wide, :], k)
            first = (
                jnp.where(wets[1], x_east - x, 0.0)
                + jnp.where(wets[2], x_west - x, 0.0)
                + jnp.where(wets[3], fields[k, wide_north, :] - x, 0.0)
                + jnp.where(wets[4], fields[k, wide_south, :] - x, 0.0)
            )
            laps[comp, wide, :] = jnp.where(wets[0], first, 0.0)
        wets = masks(level_float, whole, northern, southern)
        for comp in range(2):
            k = comp * count + level
            x = laps[comp, whole, :]
            x_east, x_west = sides(x, firsts[whole, :], k)
            second = weighted(x, (x_east, x_west, laps[comp, northern, :], laps[comp, southern, :]), wets, 0)
            turned = faces[2, 2, 0:rows, :] * fields[(1 - comp) * count + level, whole, :]
            star = fields[k, whole, :] - second
            star = jnp.where(wets[0], star + turned if comp == 0 else star - turned, 0.0)
            star_out[k] = star
            deep[2 + comp, 0, start:stop, :] += star
        return carry

    lax.fori_loop(0, count, velocity_level, 0)

    levels_here = flats[2, whole, :]
    ocean_here = jnp.where(levels_here > 0, 1.0, 0.0)
    for comp in range(2):
        mean = deep[2 + comp, 0, start:stop, :] / jnp.maximum(levels_here, 1.0)
        extra_out[comp] = mean
        deep[2 + comp, 0, start:stop, :] = mean + wind[comp] * ocean_here

    def flow_edge(i):
        at = stop - DEEP if i == 0 else start
        return deep.at[2:4, 0, at : at + DEEP, :]

    fold_dst = lambda i: fold_recv.at[i]
    rows_out(flow_edge, fold_dst, 3)

    def tracer_level(level, carry):
        wets = masks(level.astype(F32), whole, northern, southern)
        for comp in range(2):
            k = 2 * count + comp * count + level
            x = fields[k, whole, :]
            x_east, x_west = sides(x, near[1, whole, :], k)
            change = weighted(x, (x_east, x_west, fields[k, northern, :], fields[k, southern, :]), wets, 1)
            tracer_out[comp * count + level] = x + jnp.where(wets[0], change, 0.0)
        return carry

    early = (3 * count) // 5
    lax.fori_loop(0, early, tracer_level, 0)

    rows_in(flow_edge, fold_dst, 3)

    @pl.when(top)
    def _():
        for comp in range(2):
            turned = -mirrored(fold_recv[0, comp])
            for n in range(DEEP):
                fold_recv[0, comp, n : n + 1, :] = turned[DEEP - 1 - n : DEEP - n]

    for comp in range(2):
        deep[2 + comp, 0, stop:end, :] = fold_recv[0, comp]

    @pl.when(jnp.logical_not(bottom))
    def _():
        for comp in range(2):
            deep[2 + comp, 0, PAD:start, :] = fold_recv[1, comp]

    for comp in range(2):
        pack_strips(1, comp)
    flow_copies = cols_copies(strip_send.at[1], strip_recv.at[1], 4)
    for copy in flow_copies:
        copy.start()

    for copy in stat_copies:
        copy.wait_recv()
    for f in range(2):
        unpack_strips(0, f)
    lax.fori_loop(early, count, tracer_level, 0)
    centre = slice(PAD, end)
    up = slice(PAD + 1, end + 1)
    down = slice(PAD - 1, end - 1)
    for tile in range(2):
        ocean[tile, centre, :] = jnp.where(deep[1, tile, centre, :] > 0, 1.0, 0.0)
    totals = [floor_diag * ocean[n, centre, :] + (1.0 - ocean[n, centre, :]) for n in range(2)]
    at = 0
    for where_from in (centre, up, down):
        d = [deep[0, n, where_from, :] for n in range(2)]
        o = [ocean[n, where_from, :] for n in range(2)]
        d_sides, o_sides = lane_sides(*d), lane_sides(*o)
        moved = [(d_sides[0], o_sides[0]), (d_sides[1], o_sides[1])]
        scale = 1.0 if where_from is centre else 0.5
        moved = [(scale, a, b) for a, b in moved]
        if where_from is not centre:
            moved.append((1.0, d, o))
        for scale, d_n, o_n in moved:
            for n in range(2):
                weight = scale * 0.5 * (deep[0, n, centre, :] + d_n[n]) * ocean[n, centre, :] * o_n[n]
                weights[at, n] = weight
                totals[n] = totals[n] + weight
            at += 1
    for n in range(2):
        weights[8, n] = totals[n]
        weights[9, n] = 0.5 * flow_step * ocean[n, centre, :]
        weights[10, n] = 0.5 * slope_step * ocean[n, centre, :]

    for copy in flow_copies:
        copy.wait_recv()
    for comp in range(2):
        unpack_strips(1, comp)
    rows_sent(flow_edge, fold_dst, 3)

    def subcycle(step, carry):
        flux_east = [deep[0, n, centre, :] * deep[2, n, centre, :] for n in range(2)]
        for n in range(2):
            flux[n, centre, :] = deep[0, n, centre, :] * deep[3, n, centre, :]
        easts, wests = lane_sides(*flux_east)
        high = []
        for n in range(2):
            divergence = (easts[n] - wests[n]) + (flux[n, up, :] - flux[n, down, :])
            high.append(basis[0, n, centre, :] - weights[9, n] * divergence)
            basis[0, n, centre, :] = high[n]
        easts, wests = lane_sides(*high)
        for n in range(2):
            slope = weights[10, n]
            deep[2, n, centre, :] = deep[2, n, centre, :] - slope * (easts[n] - wests[n])
            deep[3, n, centre, :] = deep[3, n, centre, :] - slope * (
                basis[0, n, up, :] - basis[0, n, down, :]
            )
        return carry

    lax.fori_loop(0, SUBCYCLES, subcycle, 0)

    for k in range(SOLVE_ITERS):
        summed = [(weights[8, n] - SHIFTS[k]) * basis[k, n, centre, :] for n in range(2)]
        at = 0
        for where_from in (centre, up, down):
            p = [basis[k, n, where_from, :] for n in range(2)]
            terms = list(lane_sides(*p)) + ([] if where_from is centre else [p])
            for term in terms:
                for n in range(2):
                    summed[n] = summed[n] - weights[at, n] * term[n]
                at += 1
        for n in range(2):
            basis[k + 1, n, centre, :] = summed[n] * (1.0 / SCALE)

    pairs = [(i, j) for i in range(SOLVE_ITERS) for j in range(i, SOLVE_ITERS + 1)]
    inside = [basis[k, 0, start:stop, :] for k in range(SOLVE_ITERS + 1)]
    lat_parts[...] = jnp.zeros(lat_parts.shape, F32)
    for n, (i, j) in enumerate(pairs):
        lat_parts[n : n + 1, :] = jnp.sum(inside[i] * inside[j], axis=0, keepdims=True)

    def all_sum(parts, slots, sends, recvs, axis, me, size):
        copies = [
            remote(parts, slots.at[d - 1], sends.at[d - 1], recvs.at[d - 1], {axis: lax.rem(me + d, size)})
            for d in range(1, size)
        ]
        for copy in copies:
            copy.start()
        for copy in copies:
            copy.wait()
        result = parts[...]
        for d in range(1, size):
            result = result + slots[d - 1]
        return result

    lon_parts[...] = all_sum(lat_parts, lat_sums, lat_send, lat_recv, "lat", lat, n_lat)
    sums = jnp.sum(
        all_sum(lon_parts, lon_sums, lon_send, lon_recv, "lon", lon, n_lon), axis=1, keepdims=True
    )
    gram = {}
    for n, (i, j) in enumerate(pairs):
        gram[i, j] = gram[j, i] = sums[n : n + 1, :]

    def inner_product(a, b):
        result = None
        for i, x in a.items():
            for j, y in b.items():
                term = x * y * gram[i, j]
                result = term if result is None else result + term
        return result

    def image_of(a):
        result = {}
        for n, x in a.items():
            for at, value in ((n, SHIFTS[n] * x), (n + 1, SCALE * x)):
                result[at] = result[at] + value if at in result else value
        return result

    one = jnp.ones((1, 1), F32)
    residual = {0: one}
    direction = {0: one}
    answer = {}
    norm = gram[0, 0]
    for iteration in range(SOLVE_ITERS):
        image = image_of(direction)
        step = norm / inner_product(direction, image)
        for n, x in direction.items():
            answer[n] = answer[n] + step * x if n in answer else step * x
        if iteration < SOLVE_ITERS - 1:
            residual = {n: (residual[n] if n in residual else 0.0) - step * x for n, x in image.items()}
            new_norm = inner_product(residual, residual)
            ratio = new_norm / norm
            direction = {
                n: x + ratio * direction[n] if n in direction else x for n, x in residual.items()
            }
            norm = new_norm
    for tile in range(2):
        surface = None
        for n, x in answer.items():
            term = x * basis[n, tile, centre, :]
            surface = term if surface is None else surface + term
        flux[tile, centre, :] = surface

    easts, wests = lane_sides(flux[0, start:stop, :], flux[1, start:stop, :])
    slopes = (easts[0] - wests[0], flux[0, start + 1 : stop + 1, :] - flux[0, start - 1 : stop - 1, :])
    for comp, slope in enumerate(slopes):
        final = deep[2 + comp, 0, start:stop, :] - weights[10, 0, DEEP : DEEP + rows, :] * slope
        extra_out[comp] = final - extra_out[comp]
    extra_out[2] = levels_here
    extra_out[3] = flux[0, start:stop, :]
    rows_sent(row_src, row_dst, 0)
    for copy in col_copies + stat_copies + flow_copies:
        copy.wait_send()


def finish(tracer_ref, star_ref, extra_ref, tracer_out, velocity_out, surface_out, corrected, sems):
    count = star_ref.shape[0] // 2
    copies = [
        pltpu.make_async_copy(tracer_ref, tracer_out, sems.at[0]),
        pltpu.make_async_copy(extra_ref.at[3], surface_out, sems.at[1]),
    ]
    for copy in copies:
        copy.start()
    for comp in range(2):

        def correct(level, carry):
            k = comp * count + level
            wet = level.astype(F32) < extra_ref[2]
            corrected[k] = star_ref[k] + jnp.where(wet, extra_ref[comp], 0.0)
            return carry

        lax.fori_loop(0, count, correct, 0)
        part = slice(comp * count, (comp + 1) * count)
        copies.append(pltpu.make_async_copy(corrected.at[part], velocity_out.at[part], sems.at[2 + comp]))
        copies[-1].start()
    for copy in copies:
        copy.wait()


def per_device(n_lon, n_lat, tracers, velocity, active_levels, diffusivity, viscosity, ocean_depth, wind_forcing):
    _, count, rows, cols = tracers.shape
    kinds = 4 * count + 3
    packed = -(-2 * kinds // 8) * 8
    message = packed + 2 * DEEP
    tall, deep_rows = rows + 2 * PAD, rows + 2 * DEEP
    padded = deep_rows + 2 * PAD
    strip_rows = 8 * -(-(deep_rows // 8) // (cols // STRIP))
    entries = 16
    block = jax.ShapeDtypeStruct((2 * count, rows, cols), F32)
    flat = jax.ShapeDtypeStruct((rows, cols), F32)
    vmem = pl.BlockSpec(memory_space=pltpu.VMEM)
    hbm = pl.BlockSpec(memory_space=pltpu.HBM)
    out = pl.pallas_call(
        functools.partial(kernel, n_lon, n_lat),
        out_shape=(block, block, jax.ShapeDtypeStruct((4, rows, cols), F32)),
        in_specs=[hbm] * 7,
        out_specs=(vmem, vmem, vmem),
        scratch_shapes=[
            pltpu.VMEM((4 * count, tall, cols), F32),
            pltpu.VMEM((3, tall, cols), F32),
            pltpu.VMEM((rows, cols), jnp.int32),
            pltpu.VMEM((2, rows, cols), F32),
            pltpu.VMEM((2, tall, cols), F32),
            pltpu.VMEM((tall, cols), F32),
            pltpu.VMEM((2, tall, cols), F32),
            pltpu.VMEM((3, 4, tall, cols), F32),
            pltpu.VMEM((4, 2, padded, cols), F32),
            pltpu.VMEM((2, padded, cols), F32),
            pltpu.VMEM((11, 2, deep_rows, cols), F32),
            pltpu.VMEM((2, padded, cols), F32),
            pltpu.VMEM((SOLVE_ITERS + 1, 2, padded, cols), F32),
            pltpu.VMEM((2, message, cols), F32),
            pltpu.VMEM((2, message, cols), F32),
            pltpu.VMEM((2, tall, cols), F32),
            pltpu.VMEM((2, tall, cols), F32),
            pltpu.VMEM((2, 2, 2, strip_rows, cols), F32),
            pltpu.VMEM((2, 2, 2, strip_rows, cols), F32),
            pltpu.VMEM((2, 2, DEEP, cols), F32),
            pltpu.VMEM((n_lat - 1, entries, cols), F32),
            pltpu.VMEM((n_lon - 1, entries, cols), F32),
            pltpu.VMEM((entries, cols), F32),
            pltpu.VMEM((entries, cols), F32),
            pltpu.SemaphoreType.DMA((7,)),
            pltpu.SemaphoreType.DMA((5, 2)),
            pltpu.SemaphoreType.DMA((5, 2)),
            pltpu.SemaphoreType.DMA((n_lat - 1,)),
            pltpu.SemaphoreType.DMA((n_lat - 1,)),
            pltpu.SemaphoreType.DMA((n_lon - 1,)),
            pltpu.SemaphoreType.DMA((n_lon - 1,)),
        ],
        compiler_params=pltpu.CompilerParams(
            collective_id=0, has_side_effects=True, vmem_limit_bytes=32 * 1024 * 1024
        ),
    )(
        tracers.reshape(2 * count, rows, cols),
        velocity.reshape(2 * count, rows, cols),
        active_levels,
        diffusivity,
        viscosity,
        ocean_depth,
        wind_forcing,
    )
    out = pl.pallas_call(
        finish,
        out_shape=(block, block, flat),
        in_specs=[vmem] * 3,
        out_specs=(hbm, hbm, hbm),
        scratch_shapes=[pltpu.VMEM((2 * count, rows, cols), F32), pltpu.SemaphoreType.DMA((4,))],
        compiler_params=pltpu.CompilerParams(vmem_limit_bytes=16 * 1024 * 1024),
    )(*out)
    return out[0].reshape(tracers.shape), out[1].reshape(velocity.shape), out[2]


def solution(mesh):
    flat = P("lat", "lon")
    deep = P(None, None, "lat", "lon")
    return jax.shard_map(
        functools.partial(per_device, mesh.shape["lon"], mesh.shape["lat"]),
        mesh=mesh,
        in_specs=(deep, deep, flat, flat, flat, flat, P(None, "lat", "lon")),
        out_specs=(deep, deep, flat),
        check_vma=False,
    )
```

time: 44.2 us -> 41.3 us (0.934)
  local copies, waits for them, and re-layouts: 8.32 us -> 6.04 us
  Pallas kernels: 34.7 us -> 34.1 us
    unnamed x17 -> x14, local copies, waits for them, and re-layouts: 8.32 us -> 6.04 us
    pallas_call x1, Pallas kernels: 34.7 us -> 33 us  [per_device(): pl.pallas_call(functools.partial(kernel, n_lon, n_lat), out_shape=(block,...]
    pallas_call x0 -> x1, Pallas kernels: none -> 1.1 us  [per_device(): pl.pallas_call(finish, out_shape=(block, block, flat), in_specs=[vmem] *...]
where the time goes in v2:
time: 41.3 us; the launch traced here: 40.8 us
  Pallas kernels  34.1 us (83%)
  local copies, waits for them, and re-layouts  6.04 us (15%)
  between operations  0.66 us (2%)
    pallas_call x1, Pallas kernels, per_device(): pl.pallas_call(functools.partial(kernel, n_lon, n_lat), out_shape=(block,...  33 us
    unnamed x14, local copies, waits for them, and re-layouts  6.04 us
    pallas_call x1, Pallas kernels, per_device(): pl.pallas_call(finish, out_shape=(block, block, flat), in_specs=[vmem] *...  1.1 us

profile of v2, /device:TPU:0, one launch (start us, length us, event | category | flops | bytes accessed | tf_op | source)
XLA Modules:
  0.0 40.8 jit_solution(15206788969606860502)
XLA Ops:
  0.6 0.0 copy-start
  0.6 1.1 %copy-done = f32[2,10,64,128]{3,2,1,0:T(8,128)S(1)} copy-done((f32[2,10,64,128]{3,2,1,0:T(8,128)S(1)}, f32[2,10,64,128]{3,2,1,0:T(8,128)}, u32[]{:S(2)}) %copy-start) | copy-done | bytes 655384
  1.7 0.0 copy-start.1
  1.7 1.1 %copy-done.1 = f32[2,10,64,128]{3,2,1,0:T(8,128)S(1)} copy-done((f32[2,10,64,128]{3,2,1,0:T(8,128)S(1)}, f32[2,10,64,128]{3,2,1,0:T(8,128)}, u32[]{:S(2)}) %copy-start.1) | copy-done | bytes 655384
  2.8 0.0 copy-start.2
  2.8 0.8 %copy-done.2 = f32[2,64,128]{2,1,0:T(8,128)S(1)} copy-done((f32[2,64,128]{2,1,0:T(8,128)S(1)}, f32[2,64,128]{2,1,0:T(8,128)}, u32[]{:S(2)}) %copy-start.2) | copy-done | bytes 65560
  3.6 0.0 copy-start.3
  3.7 0.8 %copy-done.3 = s32[64,128]{1,0:T(8,128)S(1)} copy-done((s32[64,128]{1,0:T(8,128)S(1)}, s32[64,128]{1,0:T(8,128)}, u32[]{:S(2)}) %copy-start.3) | copy-done | bytes 32792
  4.4 0.0 copy-start.4
  4.4 0.8 %copy-done.4 = f32[64,128]{1,0:T(8,128)S(1)} copy-done((f32[64,128]{1,0:T(8,128)S(1)}, f32[64,128]{1,0:T(8,128)}, u32[]{:S(2)}) %copy-start.4) | copy-done | bytes 32792
  5.2 0.0 copy-start.5
  5.2 0.8 %copy-done.5 = f32[64,128]{1,0:T(8,128)S(1)} copy-done((f32[64,128]{1,0:T(8,128)S(1)}, f32[64,128]{1,0:T(8,128)}, u32[]{:S(2)}) %copy-start.5) | copy-done | bytes 32792
  5.9 0.0 copy-start.6
  5.9 0.8 %copy-done.6 = f32[64,128]{1,0:T(8,128)S(1)} copy-done((f32[64,128]{1,0:T(8,128)S(1)}, f32[64,128]{1,0:T(8,128)}, u32[]{:S(2)}) %copy-start.6) | copy-done | bytes 32792
  6.7 33.0 %shard_map.94 = (f32[20,64,128]{2,1,0:T(8,128)S(1)}, f32[20,64,128]{2,1,0:T(8,128)S(1)}, f32[4,64,128]{2,1,0:T(8,128)S(1)}) custom-call(f32[20,64,128]{2,1,0:T(8,128)S(1)} %bitcast.4, f32[20,64,128]{2,1,0:T(8,128)S(1)} %bitcast.5, s32[64,128]{1,0:T(8,128)S(1)} %copy-done.3, f32[64,128]{1,0:T(8,128)S(1)} %copy-done.4, f32[64,128]{1,0:T(8,128)S(1)} %copy-done.5, ...), custom_call_target="tpu_custom_call" | custom-call | tf_op jit(solution)/shard_map/pallas_call | solution.py:644
  39.7 1.1 %shard_map.95 = (f32[20,64,128]{2,1,0:T(8,128)}, f32[20,64,128]{2,1,0:T(8,128)}, f32[64,128]{1,0:T(8,128)}) custom-call(f32[20,64,128]{2,1,0:T(8,128)S(1)} %get-tuple-element.9.tracer_ref, f32[20,64,128]{2,1,0:T(8,128)S(1)} %get-tuple-element.10.star_ref, f32[4,64,128]{2,1,0:T(8,128)S(1)} %get-tuple-element.11.extra_ref), custom_call_target="tpu_custom_call" | custom-call | tf_op jit(solution)/shard_map/pallas_call | solution.py:694
Async XLA Ops:
  0.6 1.1 %copy-start = (f32[2,10,64,128]{3,2,1,0:T(8,128)S(1)}, f32[2,10,64,128]{3,2,1,0:T(8,128)}, u32[]{:S(2)}) copy-start(f32[2,10,64,128]{3,2,1,0:T(8,128)} %param.7) | copy-start | bytes 1966084
  1.7 1.1 %copy-start.1 = (f32[2,10,64,128]{3,2,1,0:T(8,128)S(1)}, f32[2,10,64,128]{3,2,1,0:T(8,128)}, u32[]{:S(2)}) copy-start(f32[2,10,64,128]{3,2,1,0:T(8,128)} %param.8) | copy-start | bytes 1966084
  2.8 0.8 %copy-start.2 = (f32[2,64,128]{2,1,0:T(8,128)S(1)}, f32[2,64,128]{2,1,0:T(8,128)}, u32[]{:S(2)}) copy-start(f32[2,64,128]{2,1,0:T(8,128)} %wind_hbm.1) | copy-start | bytes 196612
  3.6 0.8 %copy-start.3 = (s32[64,128]{1,0:T(8,128)S(1)}, s32[64,128]{1,0:T(8,128)}, u32[]{:S(2)}) copy-start(s32[64,128]{1,0:T(8,128)} %levels_hbm.1) | copy-start | bytes 98308
  4.4 0.8 %copy-start.4 = (f32[64,128]{1,0:T(8,128)S(1)}, f32[64,128]{1,0:T(8,128)}, u32[]{:S(2)}) copy-start(f32[64,128]{1,0:T(8,128)} %diff_hbm.1) | copy-start | bytes 98308
  5.2 0.8 %copy-start.5 = (f32[64,128]{1,0:T(8,128)S(1)}, f32[64,128]{1,0:T(8,128)}, u32[]{:S(2)}) copy-start(f32[64,128]{1,0:T(8,128)} %visc_hbm.1) | copy-start | bytes 98308
  5.9 0.8 %copy-start.6 = (f32[64,128]{1,0:T(8,128)S(1)}, f32[64,128]{1,0:T(8,128)}, u32[]{:S(2)}) copy-start(f32[64,128]{1,0:T(8,128)} %depth_hbm.1) | copy-start | bytes 98308

commit v3 on v2

--- a/solution.py
+++ b/solution.py
@@ -45,6 +45,16 @@
 
 def mirrored(x):
     return jnp.take_along_axis(x, x.shape[1] - 1 - lanes(x.shape), axis=1)
+
+
+def upturned(x):
+    ids = 7 - lax.broadcasted_iota(jnp.int32, (8, x.shape[1]), 0)
+    tiles = [x[at : at + 8] for at in range(0, x.shape[0], 8)]
+    return jnp.concatenate([jnp.take_along_axis(tile, ids, axis=0) for tile in tiles[::-1]], axis=0)
+
+
+def folded(x):
+    return upturned(mirrored(x))
 
 
 def kernel(
@@ -57,6 +67,9 @@
     visc_hbm,
     depth_hbm,
     wind_hbm,
+    tracer_hbm_out,
+    star_hbm_out,
+    extra_hbm_out,
     tracer_out,
     star_out,
     extra_out,
@@ -79,18 +92,19 @@
     col_recv,
     strip_send,
     strip_recv,
+    corner_send,
+    corner_recv,
     fold_recv,
-    lat_sums,
-    lon_sums,
-    lat_parts,
-    lon_parts,
+    part,
+    parts,
     load_sems,
+    store_sems,
     send_sems,
     recv_sems,
-    lat_send,
-    lat_recv,
-    lon_send,
-    lon_recv,
+    corner_send_sems,
+    corner_recv_sems,
+    sum_send,
+    sum_recv,
 ):
     count = tracer_hbm.shape[0] // 2
     rows, cols = levels_hbm.shape
@@ -132,14 +146,18 @@
         )
 
     barrier = pltpu.get_barrier_semaphore()
-    for apart in range(1, n_lon):
-        pl.semaphore_signal(
-            barrier, inc=1, device_id={"lon": lax.rem(lon + apart, n_lon)}, device_id_type=MESH
-        )
-    for apart in range(1, n_lat):
-        pl.semaphore_signal(
-            barrier, inc=1, device_id={"lat": lax.rem(lat + apart, n_lat)}, device_id_type=MESH
-        )
+
+    def peer(k):
+        return {
+            "lat": lax.rem(lat + k // n_lon, n_lat),
+            "lon": lax.rem(lon + lax.rem(k, n_lon), n_lon),
+        }
+
+    def greet(k, carry):
+        pl.semaphore_signal(barrier, inc=1, device_id=peer(k), device_id_type=MESH)
+        return carry
+
+    lax.fori_loop(1, n_lon * n_lat, greet, 0)
 
     kinds = 4 * count + 3
     packed = -(-2 * kinds // 8) * 8
@@ -153,12 +171,10 @@
         array[:, :, end:, :] = jnp.zeros((array.shape[0], 2, PAD, cols), F32)
     basis[0, :, PAD:end, :] = jnp.zeros((2, deep_rows, cols), F32)
     laps[...] = jnp.zeros(laps.shape, F32)
-    for n in range(2):
-        near[n] = jnp.zeros(near.shape[1:], F32)
-
     @pl.when(bottom)
     def _():
         row_recv[1] = jnp.zeros(row_recv.shape[1:], F32)
+        corner_recv[:, 2:4] = jnp.zeros((2, 2) + corner_recv.shape[2:], F32)
 
     for load in loads:
         load.wait()
@@ -180,7 +196,7 @@
         row_send[0, at : at + DEEP, :] = deep[f, 0, stop - DEEP : stop, :]
         row_send[1, at : at + DEEP, :] = deep[f, 0, start : start + DEEP, :]
 
-    pl.semaphore_wait(barrier, n_lon + n_lat - 2)
+    pl.semaphore_wait(barrier, n_lon * n_lat - 1)
 
     def rows_out(src, dst, stage):
         @pl.when(top)
@@ -230,8 +246,119 @@
         own = jnp.where(pair, roll(x, 2 * k + 1, 1), own)
         if k < 2 * count or k == kinds - 1:
             inner = jnp.where(pair, jnp.where(odd_here, roll(x, 2 * k, 1), roll(x, 2 * k + 2, 1)), inner)
-    near[0, PAD:top_row, :] = own
-    near[1, PAD:top_row, :] = inner
+    col_send[1] = jnp.where(odd_here, own, roll(inner, -1, 1))
+    col_send[0] = jnp.where(odd_here, roll(inner, 1, 1), own)
+    col_copies = cols_copies(col_send, col_recv, 1)
+    for copy in col_copies:
+        copy.start()
+
+    groups = cols // STRIP
+    tiles = rows // 8
+    rim_tiles = DEEP // 8
+    group_of = lanes((8, cols)) // STRIP
+
+    def strip_of(ref, base, first_row, number):
+        strip = None
+        for g in range(number):
+            at = first_row + 8 * g
+            x = roll(ref[at : at + 8, :], STRIP * g - base, 1)
+            strip = x if strip is None else jnp.where(group_of == g, x, strip)
+        return strip
+
+    def pack_strips(pair, f):
+        ref = deep.at[2 * pair + f, 0]
+        for side, base in ((0, cols - STRIP), (1, 0)):
+            for t in range(0, tiles, groups):
+                at = 8 * (t // groups)
+                strip_send[pair, side, f, at : at + 8, :] = strip_of(
+                    ref, base, start + 8 * t, min(groups, tiles - t)
+                )
+            for corner, first_row in ((side, stop - DEEP), (2 + side, start)):
+                corner_send[pair, corner, 8 * f : 8 * f + 8, :] = strip_of(ref, base, first_row, rim_tiles)
+
+    def fill(pair, f, at, west_tile, east_tile, g):
+        low = roll(east_tile, -STRIP * g, 1)
+        high = roll(west_tile, cols - STRIP - STRIP * g, 1)
+        deep[2 * pair + f, 1, at : at + 8, :] = jnp.where(group_of < groups // 2, low, high)
+
+    def unpack_strips(pair, f, sign):
+        for j in range(tiles):
+            at = 8 * (j // groups)
+            west_tile = strip_recv[pair, 0, f, at : at + 8, :]
+            east_tile = strip_recv[pair, 1, f, at : at + 8, :]
+            fill(pair, f, start + 8 * j, west_tile, east_tile, j % groups)
+        tile_at = slice(8 * f, 8 * f + 8)
+
+        @pl.when(top)
+        def _():
+            for corner in range(2):
+                tile = folded(corner_recv[pair, corner, tile_at, :])
+                corner_recv[pair, corner, tile_at, :] = sign * roll(tile, -STRIP, 1)
+
+        for j in range(rim_tiles):
+            fill(pair, f, stop + 8 * j, corner_recv[pair, 1, tile_at, :], corner_recv[pair, 0, tile_at, :], j)
+            fill(
+                pair, f, PAD + 8 * j, corner_recv[pair, 3, tile_at, :], corner_recv[pair, 2, tile_at, :], j
+            )
+
+    turned_lon = (lax.rem(2 * n_lon - 2 - lon, n_lon), lax.rem(n_lon - lon, n_lon))
+    alone = [jnp.logical_and(top, turned == lon) for turned in turned_lon]
+
+    def corner_copy(pair, corner, slot, device):
+        size = 24 if pair == 0 else 16
+        return remote(
+            corner_send.at[pair, corner, 0:size, :],
+            corner_recv.at[pair, slot, 0:size, :],
+            corner_send_sems.at[pair, corner],
+            corner_recv_sems.at[pair, slot],
+            device,
+        )
+
+    def corners_out(pair):
+        for corner in range(2):
+            side = right if corner == 0 else left
+
+            @pl.when(jnp.logical_not(top))
+            def _():
+                corner_copy(pair, corner, 3 - corner, {"lat": above, "lon": side}).start()
+
+            @pl.when(jnp.logical_and(top, turned_lon[corner] != lon))
+            def _():
+                corner_copy(pair, corner, corner, {"lon": turned_lon[corner]}).start()
+
+            @pl.when(alone[corner])
+            def _():
+                corner_recv[pair, corner] = corner_send[pair, corner]
+
+            @pl.when(jnp.logical_not(bottom))
+            def _():
+                corner_copy(pair, 2 + corner, 1 - corner, {"lat": below, "lon": side}).start()
+
+    def corners_each(pair, act):
+        for corner in range(2):
+            side = right if corner == 0 else left
+
+            @pl.when(jnp.logical_not(alone[corner]))
+            def _():
+                act(corner_copy(pair, corner, corner, {"lat": above, "lon": side}))
+
+            @pl.when(jnp.logical_not(bottom))
+            def _():
+                act(corner_copy(pair, 2 + corner, 2 + corner, {"lat": below, "lon": side}))
+
+    for corner in range(4):
+        at = rows - 8 if corner < 2 else 0
+        corner_send[0, corner, 16:24, :] = own[at : at + 8]
+    for f in range(2):
+        pack_strips(0, f)
+    corners_out(0)
+    stat_copies = cols_copies(strip_send.at[0], strip_recv.at[0], 2)
+    for copy in stat_copies:
+        copy.start()
+
+    row_ids = (lat * rows + lax.broadcasted_iota(jnp.int32, (rows, cols), 0)).astype(F32)
+    coriolis = 0.25 * jnp.sin(math.pi * ((row_ids + 0.5) / (rows * n_lat) - 0.5))
+    faces[2, 2, 0:rows, :] = coriolis
 
     rows_in(row_src, row_dst, 0)
 
@@ -243,62 +370,12 @@
         row_recv[0, 0:packed, :] = turned[0:packed]
         for f in range(2):
             at = packed + f * DEEP
-            for n in range(DEEP):
-                row_recv[0, at + n : at + n + 1, :] = turned[at + DEEP - 1 - n : at + DEEP - n]
+            row_recv[0, at : at + DEEP, :] = upturned(turned[at : at + DEEP])
 
     for f in range(2):
         at = packed + f * DEEP
         deep[f, 0, PAD:start, :] = row_recv[1, at : at + DEEP, :]
         deep[f, 0, stop:end, :] = row_recv[0, at : at + DEEP, :]
-
-    tall = rows + 2 * PAD
-    lane = lanes((tall, cols))
-    odd = jnp.bitwise_and(lane, 1) == 1
-
-    def corner(received):
-        square = jnp.concatenate([received, jnp.zeros((cols - packed, cols), F32)], axis=0)
-        turned = jnp.transpose(square)
-        return jnp.where(
-            jnp.bitwise_and(lanes((1, cols)), 1) == 1,
-            turned[0:1, :],
-            roll(turned[cols - PAD :, :], -1, 1)[PAD - 1 :, :],
-        )
-
-    near[0, PAD - 1 : PAD, :] = corner(row_recv[1, 0:packed, :])
-    near[0, top_row : top_row + 1, :] = corner(row_recv[0, 0:packed, :])
-    own, inner = near[0], near[1]
-    col_send[1] = jnp.where(odd, own, roll(inner, -1, 1))
-    col_send[0] = jnp.where(odd, roll(inner, 1, 1), own)
-    col_copies = cols_copies(col_send, col_recv, 1)
-    for copy in col_copies:
-        copy.start()
-
-    groups = cols // STRIP
-    tiles = deep_rows // 8
-    group_of = lanes((8, cols)) // STRIP
-
-    def pack_strips(pair, f):
-        for side, base in ((0, cols - STRIP), (1, 0)):
-            for t in range(0, tiles, groups):
-                strip = None
-                for g in range(min(groups, tiles - t)):
-                    at = PAD + 8 * (t + g)
-                    x = roll(deep[2 * pair + f, 0, at : at + 8, :], STRIP * g - base, 1)
-                    strip = x if strip is None else jnp.where(group_of == g, x, strip)
-                strip_send[pair, side, f, 8 * (t // groups) : 8 * (t // groups) + 8, :] = strip
-
-    def unpack_strips(pair, f):
-        for j in range(tiles):
-            at, t, g = PAD + 8 * j, 8 * (j // groups), j % groups
-            low = roll(strip_recv[pair, 1, f, t : t + 8, :], -STRIP * g, 1)
-            high = roll(strip_recv[pair, 0, f, t : t + 8, :], cols - STRIP - STRIP * g, 1)
-            deep[2 * pair + f, 1, at : at + 8, :] = jnp.where(group_of < groups // 2, low, high)
-
-    for f in range(2):
-        pack_strips(0, f)
-    stat_copies = cols_copies(strip_send.at[0], strip_recv.at[0], 2)
-    for copy in stat_copies:
-        copy.start()
 
     for k in range(kinds):
         ref, index = block_of(k)
@@ -306,16 +383,35 @@
         ref[index, top_row + 1 : top_row + 2, :] = row_recv[0, 2 * k : 2 * k + 1, :]
         ref[index, PAD - 2 : PAD, :] = row_recv[1, 2 * k : 2 * k + 2, :]
 
-    row_ids = (lat * rows + lax.broadcasted_iota(jnp.int32, (rows, cols), 0)).astype(F32)
-    coriolis = 0.25 * jnp.sin(math.pi * ((row_ids + 0.5) / (rows * n_lat) - 0.5))
-    faces[2, 2, 0:rows, :] = coriolis
-
     for copy in col_copies:
         copy.wait_recv()
+    corners_each(0, lambda copy: copy.wait_recv())
+    tall = rows + 2 * PAD
+    lane = lanes((tall, cols))
+    odd = jnp.bitwise_and(lane, 1) == 1
     from_west, from_east = col_recv[0], col_recv[1]
-    close = jnp.where(odd, roll(from_west, 1, 1), roll(from_east, -1, 1))
-    far = jnp.where(odd, from_west, from_east)
-    near[1] = close
+    near[1] = jnp.zeros((tall, cols), F32)
+    near[0] = jnp.zeros((tall, cols), F32)
+    near[1, PAD:top_row, :] = jnp.where(odd_here, roll(from_west, 1, 1), roll(from_east, -1, 1))
+    near[0, PAD:top_row, :] = jnp.where(odd_here, from_west, from_east)
+    odd_tile = jnp.bitwise_and(lanes((8, cols)), 1) == 1
+    ne, nw, se, sw = [corner_recv[0, corner, 16:24, :] for corner in range(4)]
+    below_tile = jnp.where(odd_tile, roll(sw, 1, 1), roll(se, -1, 1))
+    near[1, PAD - 1 : PAD, :] = below_tile[7:8]
+
+    @pl.when(top)
+    def _():
+        tile = jnp.where(odd_tile, nw, ne)
+        tile = jnp.where(lanes((8, cols)) < 4 * count, -tile, tile)
+        near[1, top_row : top_row + 1, :] = tile[7:8]
+
+    @pl.when(jnp.logical_not(top))
+    def _():
+        tile = jnp.where(odd_tile, roll(nw, 1, 1), roll(ne, -1, 1))
+        near[1, top_row : top_row + 1, :] = tile[0:1]
+
+    close, far = near[1], near[0]
+    own = jnp.concatenate([jnp.zeros((PAD, cols), F32), own, jnp.zeros((PAD, cols), F32)], axis=0)
 
     level_of = lax.rem(jnp.right_shift(lane, 1), count).astype(F32)
 
@@ -415,6 +511,14 @@
 
     fold_dst = lambda i: fold_recv.at[i]
     rows_out(flow_edge, fold_dst, 3)
+    for comp in range(2):
+        pack_strips(1, comp)
+    flow_copies = cols_copies(strip_send.at[1], strip_recv.at[1], 4)
+    for copy in flow_copies:
+        copy.start()
+    corners_out(1)
+    stores = [pltpu.make_async_copy(star_out, star_hbm_out, store_sems.at[0])]
+    stores[0].start()
 
     def tracer_level(level, carry):
         wets = masks(level.astype(F32), whole, northern, southern)
@@ -426,37 +530,14 @@
             tracer_out[comp * count + level] = x + jnp.where(wets[0], change, 0.0)
         return carry
 
-    early = (3 * count) // 5
-    lax.fori_loop(0, early, tracer_level, 0)
-
-    rows_in(flow_edge, fold_dst, 3)
-
-    @pl.when(top)
-    def _():
-        for comp in range(2):
-            turned = -mirrored(fold_recv[0, comp])
-            for n in range(DEEP):
-                fold_recv[0, comp, n : n + 1, :] = turned[DEEP - 1 - n : DEEP - n]
-
-    for comp in range(2):
-        deep[2 + comp, 0, stop:end, :] = fold_recv[0, comp]
-
-    @pl.when(jnp.logical_not(bottom))
-    def _():
-        for comp in range(2):
-            deep[2 + comp, 0, PAD:start, :] = fold_recv[1, comp]
-
-    for comp in range(2):
-        pack_strips(1, comp)
-    flow_copies = cols_copies(strip_send.at[1], strip_recv.at[1], 4)
-    for copy in flow_copies:
-        copy.start()
+    lax.fori_loop(0, count, tracer_level, 0)
+    stores.append(pltpu.make_async_copy(tracer_out, tracer_hbm_out, store_sems.at[1]))
+    stores[1].start()
 
     for copy in stat_copies:
         copy.wait_recv()
     for f in range(2):
-        unpack_strips(0, f)
-    lax.fori_loop(early, count, tracer_level, 0)
+        unpack_strips(0, f, 1.0)
     centre = slice(PAD, end)
     up = slice(PAD + 1, end + 1)
     down = slice(PAD - 1, end - 1)
@@ -486,8 +567,24 @@
 
     for copy in flow_copies:
         copy.wait_recv()
+    corners_each(1, lambda copy: copy.wait_recv())
+    rows_in(flow_edge, fold_dst, 3)
     for comp in range(2):
-        unpack_strips(1, comp)
+        unpack_strips(1, comp, -1.0)
+
+    @pl.when(top)
+    def _():
+        for comp in range(2):
+            fold_recv[0, comp] = -folded(fold_recv[0, comp])
+
+    for comp in range(2):
+        deep[2 + comp, 0, stop:end, :] = fold_recv[0, comp]
+
+    @pl.when(jnp.logical_not(bottom))
+    def _():
+        for comp in range(2):
+            deep[2 + comp, 0, PAD:start, :] = fold_recv[1, comp]
+
     rows_sent(flow_edge, fold_dst, 3)
 
     def subcycle(step, carry):
@@ -526,31 +623,35 @@
 
     pairs = [(i, j) for i in range(SOLVE_ITERS) for j in range(i, SOLVE_ITERS + 1)]
     inside = [basis[k, 0, start:stop, :] for k in range(SOLVE_ITERS + 1)]
-    lat_parts[...] = jnp.zeros(lat_parts.shape, F32)
+    lane_row = lanes((1, cols))
+    packed_sums = jnp.zeros((1, cols), F32)
     for n, (i, j) in enumerate(pairs):
-        lat_parts[n : n + 1, :] = jnp.sum(inside[i] * inside[j], axis=0, keepdims=True)
-
-    def all_sum(parts, slots, sends, recvs, axis, me, size):
-        copies = [
-            remote(parts, slots.at[d - 1], sends.at[d - 1], recvs.at[d - 1], {axis: lax.rem(me + d, size)})
-            for d in range(1, size)
-        ]
-        for copy in copies:
-            copy.start()
-        for copy in copies:
-            copy.wait()
-        result = parts[...]
-        for d in range(1, size):
-            result = result + slots[d - 1]
-        return result
-
-    lon_parts[...] = all_sum(lat_parts, lat_sums, lat_send, lat_recv, "lat", lat, n_lat)
-    sums = jnp.sum(
-        all_sum(lon_parts, lon_sums, lon_send, lon_recv, "lon", lon, n_lon), axis=1, keepdims=True
-    )
+        value = jnp.sum(jnp.sum(inside[i] * inside[j], axis=0, keepdims=True), axis=1, keepdims=True)
+        packed_sums = jnp.where(lane_row == n, value, packed_sums)
+    me = lat * n_lon + lon
+    part[0] = packed_sums
+    parts[me] = packed_sums
+
+    def sum_copy(k):
+        return remote(part, parts.at[pl.ds(me, 1)], sum_send.at[k], sum_recv.at[k], peer(k))
+
+    def sum_start(k, carry):
+        sum_copy(k).start()
+        return carry
+
+    def sum_wait(k, carry):
+        sum_copy(k).wait()
+        return carry
+
+    lax.fori_loop(1, n_lon * n_lat, sum_start, 0)
+    lax.fori_loop(1, n_lon * n_lat, sum_wait, 0)
+    sums = parts[0]
+    for n in range(1, n_lon * n_lat):
+        sums = sums + parts[n]
+    sums = jnp.broadcast_to(sums, (8, cols))
     gram = {}
     for n, (i, j) in enumerate(pairs):
-        gram[i, j] = gram[j, i] = sums[n : n + 1, :]
+        gram[i, j] = gram[j, i] = jnp.broadcast_to(sums[:, n : n + 1], (8, cols))
 
     def inner_product(a, b):
         result = None
@@ -567,7 +668,7 @@
                 result[at] = result[at] + value if at in result else value
         return result
 
-    one = jnp.ones((1, 1), F32)
+    one = jnp.ones((8, cols), F32)
     residual = {0: one}
     direction = {0: one}
     answer = {}
@@ -588,7 +689,7 @@
     for tile in range(2):
         surface = None
         for n, x in answer.items():
-            term = x * basis[n, tile, centre, :]
+            term = x[0:1] * basis[n, tile, centre, :]
             surface = term if surface is None else surface + term
         flux[tile, centre, :] = surface
 
@@ -599,33 +700,51 @@
         extra_out[comp] = final - extra_out[comp]
     extra_out[2] = levels_here
     extra_out[3] = flux[0, start:stop, :]
+    stores.append(pltpu.make_async_copy(extra_out, extra_hbm_out, store_sems.at[2]))
+    stores[2].start()
     rows_sent(row_src, row_dst, 0)
+    for pair in range(2):
+        corners_each(pair, lambda copy: copy.wait_send())
     for copy in col_copies + stat_copies + flow_copies:
         copy.wait_send()
-
-
-def finish(tracer_ref, star_ref, extra_ref, tracer_out, velocity_out, surface_out, corrected, sems):
-    count = star_ref.shape[0] // 2
-    copies = [
-        pltpu.make_async_copy(tracer_ref, tracer_out, sems.at[0]),
-        pltpu.make_async_copy(extra_ref.at[3], surface_out, sems.at[1]),
+    for store in stores:
+        store.wait()
+
+
+def finish(
+    tracer_hbm, star_hbm, extra_hbm, tracer_out, velocity_out, surface_out, tracer, star, extra, corrected, sems
+):
+    count = star.shape[0] // 2
+    parts = (slice(0, count), slice(count, 2 * count))
+    loads = [
+        pltpu.make_async_copy(extra_hbm, extra, sems.at[0]),
+        pltpu.make_async_copy(star_hbm.at[parts[0]], star.at[parts[0]], sems.at[1]),
+        pltpu.make_async_copy(star_hbm.at[parts[1]], star.at[parts[1]], sems.at[2]),
+        pltpu.make_async_copy(tracer_hbm, tracer, sems.at[3]),
     ]
-    for copy in copies:
-        copy.start()
+    for load in loads:
+        load.start()
+    loads[0].wait()
+    stores = [pltpu.make_async_copy(extra.at[3], surface_out, sems.at[4])]
+    stores[0].start()
     for comp in range(2):
+        loads[1 + comp].wait()
 
         def correct(level, carry):
             k = comp * count + level
-            wet = level.astype(F32) < extra_ref[2]
-            corrected[k] = star_ref[k] + jnp.where(wet, extra_ref[comp], 0.0)
+            wet = level.astype(F32) < extra[2]
+            corrected[k] = star[k] + jnp.where(wet, extra[comp], 0.0)
             return carry
 
         lax.fori_loop(0, count, correct, 0)
-        part = slice(comp * count, (comp + 1) * count)
-        copies.append(pltpu.make_async_copy(corrected.at[part], velocity_out.at[part], sems.at[2 + comp]))
-        copies[-1].start()
-    for copy in copies:
-        copy.wait()
+        store = pltpu.make_async_copy(corrected.at[parts[comp]], velocity_out.at[parts[comp]], sems.at[5 + comp])
+        store.start()
+        stores.append(store)
+    loads[3].wait()
+    stores.append(pltpu.make_async_copy(tracer, tracer_out, sems.at[7]))
+    stores[-1].start()
+    for store in stores:
+        store.wait()
 
 
 def per_device(n_lon, n_lat, tracers, velocity, active_levels, diffusivity, viscosity, ocean_depth, wind_forcing):
@@ -635,18 +754,20 @@
     message = packed + 2 * DEEP
     tall, deep_rows = rows + 2 * PAD, rows + 2 * DEEP
     padded = deep_rows + 2 * PAD
-    strip_rows = 8 * -(-(deep_rows // 8) // (cols // STRIP))
-    entries = 16
+    strip_rows = 8 * -(-(rows // 8) // (cols // STRIP))
+    extra = jax.ShapeDtypeStruct((4, rows, cols), F32)
     block = jax.ShapeDtypeStruct((2 * count, rows, cols), F32)
     flat = jax.ShapeDtypeStruct((rows, cols), F32)
-    vmem = pl.BlockSpec(memory_space=pltpu.VMEM)
     hbm = pl.BlockSpec(memory_space=pltpu.HBM)
     out = pl.pallas_call(
         functools.partial(kernel, n_lon, n_lat),
-        out_shape=(block, block, jax.ShapeDtypeStruct((4, rows, cols), F32)),
+        out_shape=(block, block, extra),
         in_specs=[hbm] * 7,
-        out_specs=(vmem, vmem, vmem),
+        out_specs=(hbm, hbm, hbm),
         scratch_shapes=[
+            pltpu.VMEM(block.shape, F32),
+            pltpu.VMEM(block.shape, F32),
+            pltpu.VMEM(extra.shape, F32),
             pltpu.VMEM((4 * count, tall, cols), F32),
             pltpu.VMEM((3, tall, cols), F32),
             pltpu.VMEM((rows, cols), jnp.int32),
@@ -662,25 +783,26 @@
             pltpu.VMEM((SOLVE_ITERS + 1, 2, padded, cols), F32),
             pltpu.VMEM((2, message, cols), F32),
             pltpu.VMEM((2, message, cols), F32),
-            pltpu.VMEM((2, tall, cols), F32),
-            pltpu.VMEM((2, tall, cols), F32),
+            pltpu.VMEM((2, rows, cols), F32),
+            pltpu.VMEM((2, rows, cols), F32),
             pltpu.VMEM((2, 2, 2, strip_rows, cols), F32),
             pltpu.VMEM((2, 2, 2, strip_rows, cols), F32),
+            pltpu.VMEM((2, 4, 24, cols), F32),
+            pltpu.VMEM((2, 4, 24, cols), F32),
             pltpu.VMEM((2, 2, DEEP, cols), F32),
-            pltpu.VMEM((n_lat - 1, entries, cols), F32),
-            pltpu.VMEM((n_lon - 1, entries, cols), F32),
-            pltpu.VMEM((entries, cols), F32),
-            pltpu.VMEM((entries, cols), F32),
+            pltpu.VMEM((1, 1, cols), F32),
+            pltpu.VMEM((n_lon * n_lat, 1, cols), F32),
             pltpu.SemaphoreType.DMA((7,)),
+            pltpu.SemaphoreType.DMA((3,)),
             pltpu.SemaphoreType.DMA((5, 2)),
             pltpu.SemaphoreType.DMA((5, 2)),
-            pltpu.SemaphoreType.DMA((n_lat - 1,)),
-            pltpu.SemaphoreType.DMA((n_lat - 1,)),
-            pltpu.SemaphoreType.DMA((n_lon - 1,)),
-            pltpu.SemaphoreType.DMA((n_lon - 1,)),
+            pltpu.SemaphoreType.DMA((2, 4)),
+            pltpu.SemaphoreType.DMA((2, 4)),
+            pltpu.SemaphoreType.DMA((n_lon * n_lat,)),
+            pltpu.SemaphoreType.DMA((n_lon * n_lat,)),
         ],
         compiler_params=pltpu.CompilerParams(
-            collective_id=0, has_side_effects=True, vmem_limit_bytes=32 * 1024 * 1024
+            collective_id=0, has_side_effects=True, vmem_limit_bytes=58 * 1024 * 1024
         ),
     )(
         tracers.reshape(2 * count, rows, cols),
@@ -694,10 +816,16 @@
     out = pl.pallas_call(
         finish,
         out_shape=(block, block, flat),
-        in_specs=[vmem] * 3,
+        in_specs=[hbm] * 3,
         out_specs=(hbm, hbm, hbm),
-        scratch_shapes=[pltpu.VMEM((2 * count, rows, cols), F32), pltpu.SemaphoreType.DMA((4,))],
-        compiler_params=pltpu.CompilerParams(vmem_limit_bytes=16 * 1024 * 1024),
+        scratch_shapes=[
+            pltpu.VMEM(block.shape, F32),
+            pltpu.VMEM(block.shape, F32),
+            pltpu.VMEM(extra.shape, F32),
+            pltpu.VMEM(block.shape, F32),
+            pltpu.SemaphoreType.DMA((8,)),
+        ],
+        compiler_params=pltpu.CompilerParams(vmem_limit_bytes=58 * 1024 * 1024),
     )(*out)
     return out[0].reshape(tracers.shape), out[1].reshape(velocity.shape), out[2]
 

time: 41.3 us -> 33.2 us (0.80)
  local copies, waits for them, and re-layouts: 6.04 us -> 0 us
  Pallas kernels: 34.1 us -> 32.4 us
    unnamed x14 -> x0, local copies, waits for them, and re-layouts: 6.04 us -> none
    pallas_call x1, Pallas kernels: 33 us -> 30.1 us  [per_device(): pl.pallas_call(functools.partial(kernel, n_lon, n_lat), out_shape=(block,...]
    pallas_call x1, Pallas kernels: 1.1 us -> 2.27 us  [per_device(): pl.pallas_call(finish, out_shape=(block, block, flat), in_specs=[hbm] * 3...]
where the time goes in v3:
time: 33.2 us; the launch traced here: 33 us
  Pallas kernels  32.4 us (98%)
  between operations  0.64 us (2%)
    pallas_call x1, Pallas kernels, per_device(): pl.pallas_call(functools.partial(kernel, n_lon, n_lat), out_shape=(block,...  30.1 us
    pallas_call x1, Pallas kernels, per_device(): pl.pallas_call(finish, out_shape=(block, block, flat), in_specs=[hbm] * 3...  2.27 us

profile of v3, /device:TPU:0, one launch (start us, length us, event | category | flops | bytes accessed | tf_op | source)
XLA Modules:
  0.0 33.0 jit_solution(10737856035026692930)
XLA Ops:
  0.6 30.1 %shard_map.94 = (f32[20,64,128]{2,1,0:T(8,128)}, f32[20,64,128]{2,1,0:T(8,128)}, f32[4,64,128]{2,1,0:T(8,128)}) custom-call(f32[20,64,128]{2,1,0:T(8,128)} %bitcast.4, f32[20,64,128]{2,1,0:T(8,128)} %bitcast.5, s32[64,128]{1,0:T(8,128)} %levels_hbm.1, f32[64,128]{1,0:T(8,128)} %diff_hbm.1, f32[64,128]{1,0:T(8,128)} %visc_hbm.1, f32[64,128]{1,0:T(8,128)} %depth_hbm.1, ...), custom_call_target="tpu_custom_call" | custom-call | tf_op jit(solution)/shard_map/pallas_call | solution.py:762
  30.8 2.3 %shard_map.95 = (f32[20,64,128]{2,1,0:T(8,128)}, f32[20,64,128]{2,1,0:T(8,128)}, f32[64,128]{1,0:T(8,128)}) custom-call(f32[20,64,128]{2,1,0:T(8,128)} %get-tuple-element.9.tracer_hbm, f32[20,64,128]{2,1,0:T(8,128)} %get-tuple-element.10.star_hbm, f32[4,64,128]{2,1,0:T(8,128)} %get-tuple-element.11.extra_hbm), custom_call_target="tpu_custom_call" | custom-call | tf_op jit(solution)/shard_map/pallas_call | solution.py:816

commit v4 on v3

--- a/solution.py
+++ b/solution.py
@@ -78,6 +78,7 @@
     levels_in,
     wind,
     near,
+    own_pack,
     firsts,
     laps,
     faces,
@@ -148,16 +149,10 @@
     barrier = pltpu.get_barrier_semaphore()
 
     def peer(k):
-        return {
-            "lat": lax.rem(lat + k // n_lon, n_lat),
-            "lon": lax.rem(lon + lax.rem(k, n_lon), n_lon),
-        }
-
-    def greet(k, carry):
+        return {"lat": lax.rem(lat + k // n_lon, n_lat), "lon": lax.rem(lon + k % n_lon, n_lon)}
+
+    for k in range(1, n_lon * n_lat):
         pl.semaphore_signal(barrier, inc=1, device_id=peer(k), device_id_type=MESH)
-        return carry
-
-    lax.fori_loop(1, n_lon * n_lat, greet, 0)
 
     kinds = 4 * count + 3
     packed = -(-2 * kinds // 8) * 8
@@ -170,7 +165,8 @@
         array[:, :, 0:PAD, :] = jnp.zeros((array.shape[0], 2, PAD, cols), F32)
         array[:, :, end:, :] = jnp.zeros((array.shape[0], 2, PAD, cols), F32)
     basis[0, :, PAD:end, :] = jnp.zeros((2, deep_rows, cols), F32)
-    laps[...] = jnp.zeros(laps.shape, F32)
+    own_pack[0:PAD, :] = jnp.zeros((PAD, cols), F32)
+    own_pack[top_row:, :] = jnp.zeros((PAD, cols), F32)
     @pl.when(bottom)
     def _():
         row_recv[1] = jnp.zeros(row_recv.shape[1:], F32)
@@ -235,19 +231,21 @@
     row_dst = lambda i: row_recv.at[i]
     rows_out(row_src, row_dst, 0)
 
-    lane = lanes((rows, cols))
-    own = jnp.zeros((rows, cols), F32)
-    inner = jnp.zeros((rows, cols), F32)
-    odd_here = jnp.bitwise_and(lane, 1) == 1
-    for k in range(kinds):
-        ref, index = block_of(k)
-        x = ref[index, PAD:top_row, :]
-        pair = jnp.right_shift(lane, 1) == k
-        own = jnp.where(pair, roll(x, 2 * k + 1, 1), own)
-        if k < 2 * count or k == kinds - 1:
-            inner = jnp.where(pair, jnp.where(odd_here, roll(x, 2 * k, 1), roll(x, 2 * k + 2, 1)), inner)
-    col_send[1] = jnp.where(odd_here, own, roll(inner, -1, 1))
-    col_send[0] = jnp.where(odd_here, roll(inner, 1, 1), own)
+    odd_tile = jnp.bitwise_and(lanes((8, cols)), 1) == 1
+    pair_of = jnp.right_shift(lanes((8, cols)), 1)
+    for at in range(0, rows, 8):
+        own = jnp.zeros((8, cols), F32)
+        inner = jnp.zeros((8, cols), F32)
+        for k in range(kinds):
+            ref, index = block_of(k)
+            x = ref[index, PAD + at : PAD + at + 8, :]
+            pair = pair_of == k
+            own = jnp.where(pair, roll(x, 2 * k + 1, 1), own)
+            if k < 2 * count or k == kinds - 1:
+                inner = jnp.where(pair, jnp.where(odd_tile, roll(x, 2 * k, 1), roll(x, 2 * k + 2, 1)), inner)
+        own_pack[PAD + at : PAD + at + 8, :] = own
+        col_send[1, at : at + 8, :] = jnp.where(odd_tile, own, roll(inner, -1, 1))
+        col_send[0, at : at + 8, :] = jnp.where(odd_tile, roll(inner, 1, 1), own)
     col_copies = cols_copies(col_send, col_recv, 1)
     for copy in col_copies:
         copy.start()
@@ -348,7 +346,7 @@
 
     for corner in range(4):
         at = rows - 8 if corner < 2 else 0
-        corner_send[0, corner, 16:24, :] = own[at : at + 8]
+        corner_send[0, corner, 16:24, :] = own_pack[PAD + at : PAD + at + 8, :]
     for f in range(2):
         pack_strips(0, f)
     corners_out(0)
@@ -392,9 +390,9 @@
     from_west, from_east = col_recv[0], col_recv[1]
     near[1] = jnp.zeros((tall, cols), F32)
     near[0] = jnp.zeros((tall, cols), F32)
+    odd_here = odd[0:rows]
     near[1, PAD:top_row, :] = jnp.where(odd_here, roll(from_west, 1, 1), roll(from_east, -1, 1))
     near[0, PAD:top_row, :] = jnp.where(odd_here, from_west, from_east)
-    odd_tile = jnp.bitwise_and(lanes((8, cols)), 1) == 1
     ne, nw, se, sw = [corner_recv[0, corner, 16:24, :] for corner in range(4)]
     below_tile = jnp.where(odd_tile, roll(sw, 1, 1), roll(se, -1, 1))
     near[1, PAD - 1 : PAD, :] = below_tile[7:8]
@@ -411,7 +409,7 @@
         near[1, top_row : top_row + 1, :] = tile[0:1]
 
     close, far = near[1], near[0]
-    own = jnp.concatenate([jnp.zeros((PAD, cols), F32), own, jnp.zeros((PAD, cols), F32)], axis=0)
+    own = own_pack[...]
 
     level_of = lax.rem(jnp.right_shift(lane, 1), count).astype(F32)
 
@@ -449,51 +447,53 @@
     faces[2, 0] = lev_east
     faces[2, 1] = lev_west
 
-    wide = slice(PAD - 1, top_row + PAD - 1)
-    wide_north = slice(PAD, top_row + PAD)
-    wide_south = slice(PAD - 2, top_row + PAD - 2)
-
-    def masks(level, here, north, south):
+    def masks(level, here):
         return (
-            level < flats[2, here, :],
-            level < faces[2, 0, here, :],
-            level < faces[2, 1, here, :],
-            level < flats[2, north, :],
-            level < flats[2, south, :],
+            level < flats[2, here : here + 8, :],
+            level < faces[2, 0, here : here + 8, :],
+            level < faces[2, 1, here : here + 8, :],
+            level < flats[2, here + 1 : here + 9, :],
+            level < flats[2, here - 1 : here + 7, :],
         )
 
-    def weighted(x, neighbours, wets, index):
+    def weighted(x, neighbours, wets, index, at):
         total = None
         for n, other in enumerate(neighbours):
-            term = faces[index, n, 0:rows, :] * jnp.where(wets[n + 1], other - x, 0.0)
+            term = faces[index, n, at : at + 8, :] * jnp.where(wets[n + 1], other - x, 0.0)
             total = term if total is None else total + term
         return total
 
     def velocity_level(level, carry):
         level_float = level.astype(F32)
-        wets = masks(level_float, wide, wide_north, wide_south)
-        for comp in range(2):
-            k = comp * count + level
-            x = fields[k, wide, :]
-            x_east, x_west = sides(x, near[1, wide, :], k)
-            first = (
-                jnp.where(wets[1], x_east - x, 0.0)
-                + jnp.where(wets[2], x_west - x, 0.0)
-                + jnp.where(wets[3], fields[k, wide_north, :] - x, 0.0)
-                + jnp.where(wets[4], fields[k, wide_south, :] - x, 0.0)
-            )
-            laps[comp, wide, :] = jnp.where(wets[0], first, 0.0)
-        wets = masks(level_float, whole, northern, southern)
-        for comp in range(2):
-            k = comp * count + level
-            x = laps[comp, whole, :]
-            x_east, x_west = sides(x, firsts[whole, :], k)
-            second = weighted(x, (x_east, x_west, laps[comp, northern, :], laps[comp, southern, :]), wets, 0)
-            turned = faces[2, 2, 0:rows, :] * fields[(1 - comp) * count + level, whole, :]
-            star = fields[k, whole, :] - second
-            star = jnp.where(wets[0], star + turned if comp == 0 else star - turned, 0.0)
-            star_out[k] = star
-            deep[2 + comp, 0, start:stop, :] += star
+        for at in range(0, rows + 8, 8):
+            here = PAD - 1 + at
+            wets = masks(level_float, here)
+            for comp in range(2):
+                k = comp * count + level
+                x = fields[k, here : here + 8, :]
+                x_east, x_west = sides(x, near[1, here : here + 8, :], k)
+                first = (
+                    jnp.where(wets[1], x_east - x, 0.0)
+                    + jnp.where(wets[2], x_west - x, 0.0)
+                    + jnp.where(wets[3], fields[k, here + 1 : here + 9, :] - x, 0.0)
+                    + jnp.where(wets[4], fields[k, here - 1 : here + 7, :] - x, 0.0)
+                )
+                laps[comp, at : at + 8, :] = jnp.where(wets[0], first, 0.0)
+        for at in range(0, rows, 8):
+            here = PAD + at
+            wets = masks(level_float, here)
+            for comp in range(2):
+                k = comp * count + level
+                x = laps[comp, at + 1 : at + 9, :]
+                x_east, x_west = sides(x, firsts[here : here + 8, :], k)
+                others = (x_east, x_west, laps[comp, at + 2 : at + 10, :], laps[comp, at : at + 8, :])
+                second = weighted(x, others, wets, 0, at)
+                other = fields[(1 - comp) * count + level, here : here + 8, :]
+                turned = faces[2, 2, at : at + 8, :] * other
+                star = fields[k, here : here + 8, :] - second
+                star = jnp.where(wets[0], star + turned if comp == 0 else star - turned, 0.0)
+                star_out[k, at : at + 8, :] = star
+                deep[2 + comp, 0, start + at : start + at + 8, :] += star
         return carry
 
     lax.fori_loop(0, count, velocity_level, 0)
@@ -521,13 +521,16 @@
     stores[0].start()
 
     def tracer_level(level, carry):
-        wets = masks(level.astype(F32), whole, northern, southern)
-        for comp in range(2):
-            k = 2 * count + comp * count + level
-            x = fields[k, whole, :]
-            x_east, x_west = sides(x, near[1, whole, :], k)
-            change = weighted(x, (x_east, x_west, fields[k, northern, :], fields[k, southern, :]), wets, 1)
-            tracer_out[comp * count + level] = x + jnp.where(wets[0], change, 0.0)
+        for at in range(0, rows, 8):
+            here = PAD + at
+            wets = masks(level.astype(F32), here)
+            for comp in range(2):
+                k = 2 * count + comp * count + level
+                x = fields[k, here : here + 8, :]
+                x_east, x_west = sides(x, near[1, here : here + 8, :], k)
+                others = (x_east, x_west, fields[k, here + 1 : here + 9, :], fields[k, here - 1 : here + 7, :])
+                change = weighted(x, others, wets, 1, at)
+                tracer_out[comp * count + level, at : at + 8, :] = x + jnp.where(wets[0], change, 0.0)
         return carry
 
     lax.fori_loop(0, count, tracer_level, 0)
@@ -538,32 +541,32 @@
         copy.wait_recv()
     for f in range(2):
         unpack_strips(0, f, 1.0)
-    centre = slice(PAD, end)
-    up = slice(PAD + 1, end + 1)
-    down = slice(PAD - 1, end - 1)
-    for tile in range(2):
-        ocean[tile, centre, :] = jnp.where(deep[1, tile, centre, :] > 0, 1.0, 0.0)
-    totals = [floor_diag * ocean[n, centre, :] + (1.0 - ocean[n, centre, :]) for n in range(2)]
-    at = 0
-    for where_from in (centre, up, down):
-        d = [deep[0, n, where_from, :] for n in range(2)]
-        o = [ocean[n, where_from, :] for n in range(2)]
-        d_sides, o_sides = lane_sides(*d), lane_sides(*o)
-        moved = [(d_sides[0], o_sides[0]), (d_sides[1], o_sides[1])]
-        scale = 1.0 if where_from is centre else 0.5
-        moved = [(scale, a, b) for a, b in moved]
-        if where_from is not centre:
-            moved.append((1.0, d, o))
-        for scale, d_n, o_n in moved:
-            for n in range(2):
-                weight = scale * 0.5 * (deep[0, n, centre, :] + d_n[n]) * ocean[n, centre, :] * o_n[n]
-                weights[at, n] = weight
+    both = range(2)
+
+    def around(ref, at):
+        result = []
+        for shift in (0, 1, -1):
+            p = [ref[n, at + shift : at + shift + 8, :] for n in both]
+            result += list(lane_sides(*p)) + ([] if shift == 0 else [p])
+        return result
+
+    scales = (1.0, 1.0, 0.5, 0.5, 1.0, 0.5, 0.5, 1.0)
+    for tile in both:
+        ocean[tile, PAD:end, :] = jnp.where(deep[1, tile, PAD:end, :] > 0, 1.0, 0.0)
+    for at in range(0, deep_rows, 8):
+        depth_here = [deep[0, n, PAD + at : PAD + at + 8, :] for n in both]
+        wet_here = [ocean[n, PAD + at : PAD + at + 8, :] for n in both]
+        totals = [floor_diag * wet_here[n] + (1.0 - wet_here[n]) for n in both]
+        sums = zip(scales, around(deep.at[0], PAD + at), around(ocean, PAD + at))
+        for index, (scale, d, o) in enumerate(sums):
+            for n in both:
+                weight = scale * 0.5 * (depth_here[n] + d[n]) * wet_here[n] * o[n]
+                weights[index, n, at : at + 8, :] = weight
                 totals[n] = totals[n] + weight
-            at += 1
-    for n in range(2):
-        weights[8, n] = totals[n]
-        weights[9, n] = 0.5 * flow_step * ocean[n, centre, :]
-        weights[10, n] = 0.5 * slope_step * ocean[n, centre, :]
+        for n in both:
+            weights[8, n, at : at + 8, :] = totals[n]
+            weights[9, n, at : at + 8, :] = 0.5 * flow_step * wet_here[n]
+            weights[10, n, at : at + 8, :] = 0.5 * slope_step * wet_here[n]
 
     for copy in flow_copies:
         copy.wait_recv()
@@ -588,45 +591,50 @@
     rows_sent(flow_edge, fold_dst, 3)
 
     def subcycle(step, carry):
-        flux_east = [deep[0, n, centre, :] * deep[2, n, centre, :] for n in range(2)]
-        for n in range(2):
-            flux[n, centre, :] = deep[0, n, centre, :] * deep[3, n, centre, :]
-        easts, wests = lane_sides(*flux_east)
-        high = []
-        for n in range(2):
-            divergence = (easts[n] - wests[n]) + (flux[n, up, :] - flux[n, down, :])
-            high.append(basis[0, n, centre, :] - weights[9, n] * divergence)
-            basis[0, n, centre, :] = high[n]
-        easts, wests = lane_sides(*high)
-        for n in range(2):
-            slope = weights[10, n]
-            deep[2, n, centre, :] = deep[2, n, centre, :] - slope * (easts[n] - wests[n])
-            deep[3, n, centre, :] = deep[3, n, centre, :] - slope * (
-                basis[0, n, up, :] - basis[0, n, down, :]
-            )
+        for at in range(0, deep_rows, 8):
+            here = slice(PAD + at, PAD + at + 8)
+            up = slice(PAD + at + 1, PAD + at + 9)
+            down = slice(PAD + at - 1, PAD + at + 7)
+            easts, wests = lane_sides(*[deep[0, n, here, :] * deep[2, n, here, :] for n in both])
+            for n in both:
+                divergence = (easts[n] - wests[n]) + (
+                    deep[0, n, up, :] * deep[3, n, up, :] - deep[0, n, down, :] * deep[3, n, down, :]
+                )
+                basis[0, n, here, :] = basis[0, n, here, :] - weights[9, n, at : at + 8, :] * divergence
+        for at in range(0, deep_rows, 8):
+            here = slice(PAD + at, PAD + at + 8)
+            easts, wests = lane_sides(*[basis[0, n, here, :] for n in both])
+            for n in both:
+                slope = weights[10, n, at : at + 8, :]
+                deep[2, n, here, :] = deep[2, n, here, :] - slope * (easts[n] - wests[n])
+                deep[3, n, here, :] = deep[3, n, here, :] - slope * (
+                    basis[0, n, PAD + at + 1 : PAD + at + 9, :] - basis[0, n, PAD + at - 1 : PAD + at + 7, :]
+                )
         return carry
 
     lax.fori_loop(0, SUBCYCLES, subcycle, 0)
 
     for k in range(SOLVE_ITERS):
-        summed = [(weights[8, n] - SHIFTS[k]) * basis[k, n, centre, :] for n in range(2)]
-        at = 0
-        for where_from in (centre, up, down):
-            p = [basis[k, n, where_from, :] for n in range(2)]
-            terms = list(lane_sides(*p)) + ([] if where_from is centre else [p])
-            for term in terms:
-                for n in range(2):
-                    summed[n] = summed[n] - weights[at, n] * term[n]
-                at += 1
-        for n in range(2):
-            basis[k + 1, n, centre, :] = summed[n] * (1.0 / SCALE)
+        for at in range(0, deep_rows, 8):
+            here = slice(PAD + at, PAD + at + 8)
+            summed = [(weights[8, n, at : at + 8, :] - SHIFTS[k]) * basis[k, n, here, :] for n in both]
+            for index, term in enumerate(around(basis.at[k], PAD + at)):
+                for n in both:
+                    summed[n] = summed[n] - weights[index, n, at : at + 8, :] * term[n]
+            for n in both:
+                basis[k + 1, n, here, :] = summed[n] * (1.0 / SCALE)
 
     pairs = [(i, j) for i in range(SOLVE_ITERS) for j in range(i, SOLVE_ITERS + 1)]
-    inside = [basis[k, 0, start:stop, :] for k in range(SOLVE_ITERS + 1)]
+    products = [None] * len(pairs)
+    for at in range(start, stop, 8):
+        inside = [basis[k, 0, at : at + 8, :] for k in range(SOLVE_ITERS + 1)]
+        for n, (i, j) in enumerate(pairs):
+            term = inside[i] * inside[j]
+            products[n] = term if products[n] is None else products[n] + term
     lane_row = lanes((1, cols))
     packed_sums = jnp.zeros((1, cols), F32)
     for n, (i, j) in enumerate(pairs):
-        value = jnp.sum(jnp.sum(inside[i] * inside[j], axis=0, keepdims=True), axis=1, keepdims=True)
+        value = jnp.sum(jnp.sum(products[n], axis=0, keepdims=True), axis=1, keepdims=True)
         packed_sums = jnp.where(lane_row == n, value, packed_sums)
     me = lat * n_lon + lon
     part[0] = packed_sums
@@ -635,16 +643,11 @@
     def sum_copy(k):
         return remote(part, parts.at[pl.ds(me, 1)], sum_send.at[k], sum_recv.at[k], peer(k))
 
-    def sum_start(k, carry):
-        sum_copy(k).start()
-        return carry
-
-    def sum_wait(k, carry):
-        sum_copy(k).wait()
-        return carry
-
-    lax.fori_loop(1, n_lon * n_lat, sum_start, 0)
-    lax.fori_loop(1, n_lon * n_lat, sum_wait, 0)
+    sum_copies = [sum_copy(k) for k in range(1, n_lon * n_lat)]
+    for copy in sum_copies:
+        copy.start()
+    for copy in sum_copies:
+        copy.wait()
     sums = parts[0]
     for n in range(1, n_lon * n_lat):
         sums = sums + parts[n]
@@ -686,12 +689,13 @@
                 n: x + ratio * direction[n] if n in direction else x for n, x in residual.items()
             }
             norm = new_norm
-    for tile in range(2):
-        surface = None
-        for n, x in answer.items():
-            term = x[0:1] * basis[n, tile, centre, :]
-            surface = term if surface is None else surface + term
-        flux[tile, centre, :] = surface
+    for at in range(start - 8, stop + 8, 8):
+        for tile in both:
+            surface = None
+            for n, x in answer.items():
+                term = x * basis[n, tile, at : at + 8, :]
+                surface = term if surface is None else surface + term
+            flux[tile, at : at + 8, :] = surface
 
     easts, wests = lane_sides(flux[0, start:stop, :], flux[1, start:stop, :])
     slopes = (easts[0] - wests[0], flux[0, start + 1 : stop + 1, :] - flux[0, start - 1 : stop - 1, :])
@@ -773,6 +777,7 @@
             pltpu.VMEM((rows, cols), jnp.int32),
             pltpu.VMEM((2, rows, cols), F32),
             pltpu.VMEM((2, tall, cols), F32),
+            pltpu.VMEM((tall, cols), F32),
             pltpu.VMEM((tall, cols), F32),
             pltpu.VMEM((2, tall, cols), F32),
             pltpu.VMEM((3, 4, tall, cols), F32),

time: 33.2 us -> 32 us (0.964)
  Pallas kernels: 32.4 us -> 31.2 us
    pallas_call x1, Pallas kernels: 30.1 us -> 28.9 us  [per_device(): pl.pallas_call(functools.partial(kernel, n_lon, n_lat), out_shape=(block,...]
where the time goes in v4:
time: 32 us; the launch traced here: 31.8 us
  Pallas kernels  31.2 us (98%)
  between operations  0.64 us (2%)
    pallas_call x1, Pallas kernels, per_device(): pl.pallas_call(functools.partial(kernel, n_lon, n_lat), out_shape=(block,...  28.9 us
    pallas_call x1, Pallas kernels, per_device(): pl.pallas_call(finish, out_shape=(block, block, flat), in_specs=[hbm] * 3...  2.27 us

profile of v4, /device:TPU:0, one launch (start us, length us, event | category | flops | bytes accessed | tf_op | source)
XLA Modules:
  0.0 31.8 jit_solution(16768056899842778459)
XLA Ops:
  0.6 28.9 %shard_map.94 = (f32[20,64,128]{2,1,0:T(8,128)}, f32[20,64,128]{2,1,0:T(8,128)}, f32[4,64,128]{2,1,0:T(8,128)}) custom-call(f32[20,64,128]{2,1,0:T(8,128)} %bitcast.4, f32[20,64,128]{2,1,0:T(8,128)} %bitcast.5, s32[64,128]{1,0:T(8,128)} %levels_hbm.1, f32[64,128]{1,0:T(8,128)} %diff_hbm.1, f32[64,128]{1,0:T(8,128)} %visc_hbm.1, f32[64,128]{1,0:T(8,128)} %depth_hbm.1, ...), custom_call_target="tpu_custom_call" | custom-call | tf_op jit(solution)/shard_map/pallas_call | solution.py:766
  29.6 2.3 %shard_map.95 = (f32[20,64,128]{2,1,0:T(8,128)}, f32[20,64,128]{2,1,0:T(8,128)}, f32[64,128]{1,0:T(8,128)}) custom-call(f32[20,64,128]{2,1,0:T(8,128)} %get-tuple-element.9.tracer_hbm, f32[20,64,128]{2,1,0:T(8,128)} %get-tuple-element.10.star_hbm, f32[4,64,128]{2,1,0:T(8,128)} %get-tuple-element.11.extra_hbm), custom_call_target="tpu_custom_call" | custom-call | tf_op jit(solution)/shard_map/pallas_call | solution.py:821

commit v5 on v4

--- a/solution.py
+++ b/solution.py
@@ -155,8 +155,6 @@
         pl.semaphore_signal(barrier, inc=1, device_id=peer(k), device_id_type=MESH)
 
     kinds = 4 * count + 3
-    packed = -(-2 * kinds // 8) * 8
-    row_send[:, 2 * kinds : packed, :] = jnp.zeros((2, packed - 2 * kinds, cols), F32)
     deep[2:4] = jnp.zeros((2,) + deep.shape[1:], F32)
     for array in (flux, ocean):
         array[:, 0:PAD, :] = jnp.zeros((2, PAD, cols), F32)
@@ -170,6 +168,7 @@
     @pl.when(bottom)
     def _():
         row_recv[1] = jnp.zeros(row_recv.shape[1:], F32)
+        deep[0:2, 0, PAD:start, :] = jnp.zeros((2, DEEP, cols), F32)
         corner_recv[:, 2:4] = jnp.zeros((2, 2) + corner_recv.shape[2:], F32)
 
     for load in loads:
@@ -182,15 +181,21 @@
     def block_of(k):
         return (fields, k) if k < 4 * count else (flats, k - 4 * count)
 
+    def row_of(k):
+        if k < 2 * count:
+            return 2 * k + 1, True
+        if k == kinds - 1:
+            return 4 * count + 1, True
+        return 2 * count + 2 + k, False
+
     for k in range(kinds):
         ref, index = block_of(k)
-        row_send[0, 2 * k : 2 * k + 2, :] = ref[index, top_row - 2 : top_row, :]
-        row_send[1, 2 * k : 2 * k + 1, :] = ref[index, PAD + 1 : PAD + 2, :]
-        row_send[1, 2 * k + 1 : 2 * k + 2, :] = ref[index, PAD : PAD + 1, :]
-    for f in range(2):
-        at = packed + f * DEEP
-        row_send[0, at : at + DEEP, :] = deep[f, 0, stop - DEEP : stop, :]
-        row_send[1, at : at + DEEP, :] = deep[f, 0, start : start + DEEP, :]
+        at, both_rows = row_of(k)
+        row_send[0, at : at + 1, :] = ref[index, top_row - 1 : top_row, :]
+        row_send[1, at : at + 1, :] = ref[index, PAD : PAD + 1, :]
+        if both_rows:
+            row_send[0, at - 1 : at, :] = ref[index, top_row - 2 : top_row - 1, :]
+            row_send[1, at - 1 : at, :] = ref[index, PAD + 1 : PAD + 2, :]
 
     pl.semaphore_wait(barrier, n_lon * n_lat - 1)
 
@@ -354,6 +359,28 @@
     for copy in stat_copies:
         copy.start()
 
+    def edge_of(pair, i):
+        at = stop - DEEP if i == 0 else start
+        return deep.at[2 * pair : 2 * pair + 2, 0, at : at + DEEP, :]
+
+    stat_edge = lambda i: edge_of(0, i)
+    stat_dst = lambda i: fold_recv.at[0, i]
+    rows_out(stat_edge, stat_dst, 5)
+
+    def place_rows(pair, sign):
+        @pl.when(top)
+        def _():
+            for f in range(2):
+                fold_recv[pair, 0, f] = sign * folded(fold_recv[pair, 0, f])
+
+        for f in range(2):
+            deep[2 * pair + f, 0, stop:end, :] = fold_recv[pair, 0, f]
+
+        @pl.when(jnp.logical_not(bottom))
+        def _():
+            for f in range(2):
+                deep[2 * pair + f, 0, PAD:start, :] = fold_recv[pair, 1, f]
+
     row_ids = (lat * rows + lax.broadcasted_iota(jnp.int32, (rows, cols), 0)).astype(F32)
     coriolis = 0.25 * jnp.sin(math.pi * ((row_ids + 0.5) / (rows * n_lat) - 0.5))
     faces[2, 2, 0:rows, :] = coriolis
@@ -365,21 +392,16 @@
         turned = mirrored(row_recv[0])
         ids = lax.broadcasted_iota(jnp.int32, turned.shape, 0)
         turned = jnp.where(ids < 4 * count, -turned, turned)
-        row_recv[0, 0:packed, :] = turned[0:packed]
-        for f in range(2):
-            at = packed + f * DEEP
-            row_recv[0, at : at + DEEP, :] = upturned(turned[at : at + DEEP])
-
-    for f in range(2):
-        at = packed + f * DEEP
-        deep[f, 0, PAD:start, :] = row_recv[1, at : at + DEEP, :]
-        deep[f, 0, stop:end, :] = row_recv[0, at : at + DEEP, :]
+        row_recv[0] = turned
 
     for k in range(kinds):
         ref, index = block_of(k)
-        ref[index, top_row : top_row + 1, :] = row_recv[0, 2 * k + 1 : 2 * k + 2, :]
-        ref[index, top_row + 1 : top_row + 2, :] = row_recv[0, 2 * k : 2 * k + 1, :]
-        ref[index, PAD - 2 : PAD, :] = row_recv[1, 2 * k : 2 * k + 2, :]
+        at, both_rows = row_of(k)
+        ref[index, top_row : top_row + 1, :] = row_recv[0, at : at + 1, :]
+        ref[index, PAD - 1 : PAD, :] = row_recv[1, at : at + 1, :]
+        if both_rows:
+            ref[index, top_row + 1 : top_row + 2, :] = row_recv[0, at - 1 : at, :]
+            ref[index, PAD - 2 : PAD - 1, :] = row_recv[1, at - 1 : at, :]
 
     for copy in col_copies:
         copy.wait_recv()
@@ -505,11 +527,8 @@
         extra_out[comp] = mean
         deep[2 + comp, 0, start:stop, :] = mean + wind[comp] * ocean_here
 
-    def flow_edge(i):
-        at = stop - DEEP if i == 0 else start
-        return deep.at[2:4, 0, at : at + DEEP, :]
-
-    fold_dst = lambda i: fold_recv.at[i]
+    flow_edge = lambda i: edge_of(1, i)
+    fold_dst = lambda i: fold_recv.at[1, i]
     rows_out(flow_edge, fold_dst, 3)
     for comp in range(2):
         pack_strips(1, comp)
@@ -539,6 +558,8 @@
 
     for copy in stat_copies:
         copy.wait_recv()
+    rows_in(stat_edge, stat_dst, 5)
+    place_rows(0, 1.0)
     for f in range(2):
         unpack_strips(0, f, 1.0)
     both = range(2)
@@ -575,19 +596,7 @@
     for comp in range(2):
         unpack_strips(1, comp, -1.0)
 
-    @pl.when(top)
-    def _():
-        for comp in range(2):
-            fold_recv[0, comp] = -folded(fold_recv[0, comp])
-
-    for comp in range(2):
-        deep[2 + comp, 0, stop:end, :] = fold_recv[0, comp]
-
-    @pl.when(jnp.logical_not(bottom))
-    def _():
-        for comp in range(2):
-            deep[2 + comp, 0, PAD:start, :] = fold_recv[1, comp]
-
+    place_rows(1, -1.0)
     rows_sent(flow_edge, fold_dst, 3)
 
     def subcycle(step, carry):
@@ -638,19 +647,16 @@
         packed_sums = jnp.where(lane_row == n, value, packed_sums)
     me = lat * n_lon + lon
     part[0] = packed_sums
-    parts[me] = packed_sums
-
-    def sum_copy(k):
-        return remote(part, parts.at[pl.ds(me, 1)], sum_send.at[k], sum_recv.at[k], peer(k))
-
-    sum_copies = [sum_copy(k) for k in range(1, n_lon * n_lat)]
-    for copy in sum_copies:
-        copy.start()
-    for copy in sum_copies:
-        copy.wait()
-    sums = parts[0]
-    for n in range(1, n_lon * n_lat):
-        sums = sums + parts[n]
+
+    others = n_lon * n_lat - 1
+    for k in range(1, others + 1):
+        remote(part, parts.at[pl.ds(me, 1)], sum_send.at[0], sum_recv.at[0], peer(k)).start()
+    every = parts.at[0:others]
+    remote(every, every, sum_send.at[0], sum_recv.at[0], peer(1)).wait_recv()
+    sums = None
+    for n in range(others + 1):
+        term = jnp.where(me == n, packed_sums, parts[n])
+        sums = term if sums is None else sums + term
     sums = jnp.broadcast_to(sums, (8, cols))
     gram = {}
     for n, (i, j) in enumerate(pairs):
@@ -706,7 +712,9 @@
     extra_out[3] = flux[0, start:stop, :]
     stores.append(pltpu.make_async_copy(extra_out, extra_hbm_out, store_sems.at[2]))
     stores[2].start()
+    remote(every, every, sum_send.at[0], sum_recv.at[0], peer(1)).wait_send()
     rows_sent(row_src, row_dst, 0)
+    rows_sent(stat_edge, stat_dst, 5)
     for pair in range(2):
         corners_each(pair, lambda copy: copy.wait_send())
     for copy in col_copies + stat_copies + flow_copies:
@@ -753,9 +761,7 @@
 
 def per_device(n_lon, n_lat, tracers, velocity, active_levels, diffusivity, viscosity, ocean_depth, wind_forcing):
     _, count, rows, cols = tracers.shape
-    kinds = 4 * count + 3
-    packed = -(-2 * kinds // 8) * 8
-    message = packed + 2 * DEEP
+    message = -(-(6 * count + 4) // 8) * 8
     tall, deep_rows = rows + 2 * PAD, rows + 2 * DEEP
     padded = deep_rows + 2 * PAD
     strip_rows = 8 * -(-(rows // 8) // (cols // STRIP))
@@ -794,17 +800,17 @@
             pltpu.VMEM((2, 2, 2, strip_rows, cols), F32),
             pltpu.VMEM((2, 4, 24, cols), F32),
             pltpu.VMEM((2, 4, 24, cols), F32),
-            pltpu.VMEM((2, 2, DEEP, cols), F32),
+            pltpu.VMEM((2, 2, 2, DEEP, cols), F32),
             pltpu.VMEM((1, 1, cols), F32),
             pltpu.VMEM((n_lon * n_lat, 1, cols), F32),
             pltpu.SemaphoreType.DMA((7,)),
             pltpu.SemaphoreType.DMA((3,)),
-            pltpu.SemaphoreType.DMA((5, 2)),
-            pltpu.SemaphoreType.DMA((5, 2)),
+            pltpu.SemaphoreType.DMA((6, 2)),
+            pltpu.SemaphoreType.DMA((6, 2)),
             pltpu.SemaphoreType.DMA((2, 4)),
             pltpu.SemaphoreType.DMA((2, 4)),
-            pltpu.SemaphoreType.DMA((n_lon * n_lat,)),
-            pltpu.SemaphoreType.DMA((n_lon * n_lat,)),
+            pltpu.SemaphoreType.DMA((1,)),
+            pltpu.SemaphoreType.DMA((1,)),
         ],
         compiler_params=pltpu.CompilerParams(
             collective_id=0, has_side_effects=True, vmem_limit_bytes=58 * 1024 * 1024

time: 32 us -> 30.5 us (0.953)
  Pallas kernels: 31.2 us -> 29.7 us
    pallas_call x1, Pallas kernels: 28.9 us -> 27.4 us  [per_device(): pl.pallas_call(functools.partial(kernel, n_lon, n_lat), out_shape=(block,...]
where the time goes in v5:
time: 30.5 us; the launch traced here: 30.3 us
  Pallas kernels  29.7 us (97%)
  between operations  0.64 us (2%)
    pallas_call x1, Pallas kernels, per_device(): pl.pallas_call(functools.partial(kernel, n_lon, n_lat), out_shape=(block,...  27.4 us
    pallas_call x1, Pallas kernels, per_device(): pl.pallas_call(finish, out_shape=(block, block, flat), in_specs=[hbm] * 3...  2.27 us

profile of v5, /device:TPU:0, one launch (start us, length us, event | category | flops | bytes accessed | tf_op | source)
XLA Modules:
  0.0 30.3 jit_solution(9715764927302104123)
XLA Ops:
  0.6 27.4 %shard_map.94 = (f32[20,64,128]{2,1,0:T(8,128)}, f32[20,64,128]{2,1,0:T(8,128)}, f32[4,64,128]{2,1,0:T(8,128)}) custom-call(f32[20,64,128]{2,1,0:T(8,128)} %bitcast.4, f32[20,64,128]{2,1,0:T(8,128)} %bitcast.5, s32[64,128]{1,0:T(8,128)} %levels_hbm.1, f32[64,128]{1,0:T(8,128)} %diff_hbm.1, f32[64,128]{1,0:T(8,128)} %visc_hbm.1, f32[64,128]{1,0:T(8,128)} %depth_hbm.1, ...), custom_call_target="tpu_custom_call" | custom-call | tf_op jit(solution)/shard_map/pallas_call | solution.py:772
  28.1 2.3 %shard_map.95 = (f32[20,64,128]{2,1,0:T(8,128)}, f32[20,64,128]{2,1,0:T(8,128)}, f32[64,128]{1,0:T(8,128)}) custom-call(f32[20,64,128]{2,1,0:T(8,128)} %get-tuple-element.9.tracer_hbm, f32[20,64,128]{2,1,0:T(8,128)} %get-tuple-element.10.star_hbm, f32[4,64,128]{2,1,0:T(8,128)} %get-tuple-element.11.extra_hbm), custom_call_target="tpu_custom_call" | custom-call | tf_op jit(solution)/shard_map/pallas_call | solution.py:827
